TPU v7x, 32 devices: a whole 2x2x4 slice. The times are simulated.
32 devices in a mesh: seq: 16 (over z, x, core), head: 2 (over y).
Axes of the slice: x: 2, y: 2, z: 4, core: 2. Of those that a mesh axis runs over, the one named last changes fastest.
Arguments:
- queries: float32 [6144, 1024], P('seq', 'head'), may hold values from -1.75 to 1.75
- key_vectors: float32 [6144, 1024], P('seq', 'head'), may hold values from -1.75 to 1.75
- value_vectors: float32 [6144, 1024], P('seq', 'head'), may hold values from -6 to 6
- out_grad: float32 [6144, 1024], P('seq', 'head'), may hold values from -6 to 6
- norm_gain: float32 [1024], P('head'), may hold values from 0.5 to 1.5
- decay_rates: float32 [8], P('head'), may hold values from 1.6276042e-06 to 0.05
- segment_ids: int32 [6144], P('seq'), may hold values from 0 to 5, never falling along the last dimension, each value on 1 to 2048 neighbouring positions
Outputs:
- query_grad: bfloat16 [6144, 1024], P('seq', 'head')
- key_grad: bfloat16 [6144, 1024], P('seq', 'head')
- value_grad: bfloat16 [6144, 1024], P('seq', 'head')
- gain_grad: float32 [1024], P('head')
Inputs may be any that keep to these rules, and one draw needn't show every extreme that they name: `segment_ids`: segment numbers never fall along the tokens; each of the 6 segments is one run of 1 to 2048 tokens, and one has exactly 2048.
All inputs are finite; a program needn't handle non-finite values.
Results may differ from a plain program's by a relative error of at most 0.001.
Values sent between devices are 32-bit elements; how exact they have to be, the bound alone decides.
A program may use at most 128 MiB of HBM per device.

v0:
```python
import jax
import jax.numpy as jnp
from jax import lax
from jax.sharding import PartitionSpec as P

HEAD_DIM = 128


PRECISE = lax.Precision.HIGHEST
EPSILON = 1e-06


def block_tables(segs, rates):
    length = segs.shape[0]
    places = jnp.arange(length, dtype=jnp.float32)
    first_seg = segs[0]
    last_seg = segs[length - 1]
    distance = places[:, None] - places[None, :]
    causal = (distance >= 0.0) & (segs[:, None] == segs[None, :])
    weights = jnp.where(
        causal[None], jnp.exp(-rates[:, None, None] * jnp.maximum(distance, 0.0)[None]), 0.0
    )
    head_first = (segs == first_seg).astype(jnp.float32)
    tail_last = (segs == last_seg).astype(jnp.float32)
    carry_in_w = jnp.exp(-rates[None, :] * (places[:, None] + 1.0)) * head_first[:, None]
    carry_out_w = jnp.exp(-rates[None, :] * (length - 1.0 - places[:, None])) * tail_last[:, None]
    back_in = jnp.exp(-rates[None, :] * (length - places[:, None])) * tail_last[:, None]
    back_out = jnp.exp(-rates[None, :] * places[:, None]) * head_first[:, None]
    multiplier = jnp.exp(-rates * length) * (first_seg == last_seg).astype(jnp.float32)
    return (weights, carry_in_w, carry_out_w, back_in, back_out, multiplier)


def weighted_carry(states_all, bounds_all, my_index, own_seg, rates, length, later):
    block_ids = jnp.arange(states_all.shape[0], dtype=jnp.int32)
    if later:
        block_gap = jnp.maximum(block_ids - my_index - 1, 0).astype(jnp.float32)
        alive_mask = (block_ids > my_index) & (bounds_all == own_seg)
    else:
        block_gap = jnp.maximum(my_index - 1 - block_ids, 0).astype(jnp.float32)
        alive_mask = (block_ids < my_index) & (bounds_all == own_seg)
    factor = jnp.where(
        alive_mask[:, None], jnp.exp(-rates[None, :] * float(length) * block_gap[:, None]), 0.0
    )
    return jnp.einsum("nh,nhde->hde", factor, states_all, precision=PRECISE)


def body(queries, key_vectors, value_vectors, out_grad, norm_gain, decay_rates, segment_ids):
    length = queries.shape[0]
    head_count = queries.shape[1] // HEAD_DIM
    features = float(head_count * HEAD_DIM * lax.axis_size("head"))
    query_rows = queries.reshape(length, head_count, HEAD_DIM)
    key_rows = key_vectors.reshape(length, head_count, HEAD_DIM)
    value_rows = value_vectors.reshape(length, head_count, HEAD_DIM)
    weights, carry_in_w, carry_out_w, back_in, back_out, multiplier = block_tables(
        segment_ids, decay_rates
    )
    first_seg = segment_ids[0:1].astype(jnp.float32)
    last_seg = segment_ids[length - 1 : length].astype(jnp.float32)
    my_index = lax.axis_index("seq")
    state_loc = jnp.einsum(
        "jhd,jhe->hde", key_rows * carry_out_w[:, :, None], value_rows, precision=PRECISE
    )
    states_all, leaves_all = (
        lax.all_gather(state_loc[None], "seq", axis=0, tiled=True),
        lax.all_gather(last_seg, "seq", axis=0, tiled=True),
    )
    carry_in = weighted_carry(
        states_all, leaves_all, my_index, first_seg[0], decay_rates, length, False
    )
    scores = jnp.einsum("ihd,jhd->hij", query_rows, key_rows, precision=PRECISE) * weights
    outputs = jnp.einsum("hij,jhd->ihd", scores, value_rows, precision=PRECISE)
    outputs = outputs + carry_in_w[:, :, None] * jnp.einsum(
        "ihd,hde->ihe", query_rows, carry_in, precision=PRECISE
    )
    flat_out = outputs.reshape(length, head_count * HEAD_DIM)
    shaped = out_grad * norm_gain[None, :]
    square_part = jnp.sum(flat_out * flat_out, axis=1)
    product_part = jnp.sum(shaped * flat_out, axis=1)
    squares, product = lax.psum((square_part, product_part), "head")
    inv_rms = lax.rsqrt(squares / features + EPSILON)
    coef_rms = inv_rms**3 * (product / features)
    grad_flat = inv_rms[:, None] * shaped - coef_rms[:, None] * flat_out
    gain_part = jnp.sum(out_grad * flat_out * inv_rms[:, None], axis=0)
    gain_grad = lax.psum(gain_part, "seq")
    grad_heads = grad_flat.reshape(length, head_count, HEAD_DIM)
    mixed = jnp.einsum("ihe,jhe->hij", grad_heads, value_rows, precision=PRECISE) * weights
    query_grad = jnp.einsum("hij,jhd->ihd", mixed, key_rows, precision=PRECISE)
    query_grad = query_grad + carry_in_w[:, :, None] * jnp.einsum(
        "ihe,hde->ihd", grad_heads, carry_in, precision=PRECISE
    )
    back_loc = jnp.einsum(
        "thd,the->hde", query_rows * back_out[:, :, None], grad_heads, precision=PRECISE
    )
    backs_all, entries_all = (
        lax.all_gather(back_loc[None], "seq", axis=0, tiled=True),
        lax.all_gather(first_seg, "seq", axis=0, tiled=True),
    )
    carry_back = weighted_carry(
        backs_all, entries_all, my_index, last_seg[0], decay_rates, length, True
    )
    key_grad = jnp.einsum("hij,ihd->jhd", mixed, query_rows, precision=PRECISE)
    key_grad = key_grad + back_in[:, :, None] * jnp.einsum(
        "jhe,hde->jhd", value_rows, carry_back, precision=PRECISE
    )
    value_grad = jnp.einsum("hij,ihe->jhe", scores, grad_heads, precision=PRECISE)
    value_grad = value_grad + back_in[:, :, None] * jnp.einsum(
        "jhd,hde->jhe", key_rows, carry_back, precision=PRECISE
    )
    width = head_count * HEAD_DIM
    return (
        query_grad.reshape(length, width).astype(jnp.bfloat16),
        key_grad.reshape(length, width).astype(jnp.bfloat16),
        value_grad.reshape(length, width).astype(jnp.bfloat16),
        gain_grad,
    )


def solution(mesh):
    return jax.shard_map(
        body,
        mesh=mesh,
        in_specs=(
            P("seq", "head"),
            P("seq", "head"),
            P("seq", "head"),
            P("seq", "head"),
            P("head"),
            P("head"),
            P("seq"),
        ),
        out_specs=(P("seq", "head"), P("seq", "head"), P("seq", "head"), P("head")),
        check_vma=False,
    )
```

profile of v0, /device:TPU:0, one launch (start us, length us, event | category | flops | bytes accessed | tf_op | source)
XLA Modules:
  0.0 173.4 jit_solution(15202231620268711860)
XLA Ops:
  7.2 0.0 all-gather.5.cloned.1.call-start
  7.3 0.8 broadcast_multiply_fusion
  8.0 1.3 fusion.79
  9.4 1.4 copy.101
  10.8 2.0 %compare_convert_fusion.1 = (f32[384]{0:T(512)S(1)}, f32[384]{0:T(512)S(1)}) fusion(s32[384]{0:T(512)} %param.13, s32[]{:T(128)} %bitcast.3, s32[]{:T(128)} %bitcast.7), kind=kLoop, calls=%fused_computation.88 | loop fusion | flops 1536 | bytes 4616 | tf_op jit(solution)/shard_map/convert_element_type | solution.py:23
  12.8 0.7 exponential_multiply_fusion.1
  13.5 1.6 fusion.55
  15.1 0.0 all-gather.7.cloned.1.call-start
  15.2 0.6 dynamic-slice
  15.7 0.7 convert_dynamic-update-slice_fusion.1
  16.5 35.4 %all-reduce = f32[16]{0:T(128)S(1)} all-reduce(f32[16]{0:T(128)S(1)} %convert_dynamic-update-slice_fusion.1), channel_id=1, replica_groups=mesh['seq'=16,'head'=2] {'seq'}, use_global_device_ids=true, to_apply=%add | all-reduce | flops 16 | bytes 128
  52.5 0.1 select_bitcast_fusion.1
  52.6 0.7 copy.59
  53.3 1.2 copy.71
  54.5 0.1 fusion.69
  54.6 0.2 fusion.71
  54.8 4.0 %fusion.58 = f32[4,384,384]{2,1,0:T(8,128)S(1)} fusion(f32[384,4,128]{0,2,1:T(8,128)} %bitcast.111, f32[384,512]{1,0:T(8,128)} %param.8), kind=kOutput, calls=%fused_computation.52 | convolution fusion | flops 905969664 | bytes 3932160 | tf_op jit(solution)/shard_map/ihd,jhd->hij/dot_general | solution.py:70
  58.9 4.0 %fusion.18 = f32[384,4,128]{0,2,1:T(8,128)} fusion(f32[4,384,384]{2,1,0:T(8,128)S(1)} %fusion.58, f32[384,384]{1,0:T(8,128)S(1)} %fusion.69, f32[4]{0:T(128)S(1)} %get-tuple-element.27, pred[384,384]{1,0:T(8,128)(4,1)S(1)} %fusion.71, f32[384,512]{1,0:T(8,128)S(1)} %copy-done), kind=kOutput, calls=%fused_computation.12 | convolution fusion | flops 907739136 | bytes 4669456 | tf_op jit(solution)/shard_map/hij,jhd->ihd/dot_general | solution.py:71
  62.8 5.8 %all-gather.5.cloned.1.call-done = f32[64,128,128]{2,1,0:T(8,128)} async-done(((f32[4,128,128]{2,1,0:T(8,128)}), f32[64,128,128]{2,1,0:T(8,128)}) %all-gather.5.cloned.1.call-update) | async-done | bytes 4194320 | tf_op jit(solution)/shard_map/all_gather | solution.py:64
  68.7 6.6 %fusion = f32[4,1,128,128]{3,1,2,0:T(1,128)S(1)} fusion(f32[16,4,1,1]{0,2,3,1:T(1,128)} %copy.59, f32[16,4,128,128]{3,2,1,0:T(8,128)} %bitcast.117), kind=kOutput, calls=%fused_computation.1 | convolution fusion | flops 12582912 | bytes 4456704 | tf_op jit(solution)/shard_map/nh,nhde->hde/dot_general | solution.py:44
  75.3 2.4 %multiply_reduce_fusion.3 = (f32[384]{0:T(512)}, f32[384,4,128]{0,2,1:T(8,128)}) fusion(f32[384,4,128]{0,2,1:T(8,128)S(1)} %copy-done.13, f32[4,128,128]{2,1,0:T(8,128)S(1)} %bitcast.120, f32[384,4,128]{0,2,1:T(8,128)S(1)} %bitcast.113, f32[384,4]{0,1:T(4,128)S(1)} %copy-done.16), kind=kOutput, calls=%fused_computation.59 | convolution fusion | flops 302775936 | bytes 2629120 | tf_op jit(solution)/shard_map/ihd,hde->ihe/dot_general | solution.py:72
  77.7 5.8 %psum.21 = f32[384]{0:T(512)} all-reduce(f32[384]{0:T(512)} %get-tuple-element.28), channel_id=1, replica_groups=mesh['seq'=16,'head'=2] {'head'}, use_global_device_ids=true, to_apply=%region_1.2 | all-reduce | flops 384 | bytes 3072 | tf_op jit(solution)/shard_map/psum | solution.py:79
  83.5 2.3 %copy.42 = f32[384,512]{1,0:T(8,128)} copy(f32[384,512]{0,1:T(8,128)} %bitcast.119) | data formatting | bytes 1572864 | tf_op jit(solution)/shard_map/reshape | solution.py:75
  85.8 0.7 add_rsqrt_fusion
  86.5 0.6 copy-done.19
  87.1 2.2 %multiply_reduce_fusion.1 = (f32[512]{0:T(512)}, f32[384]{0:T(512)}) fusion(f32[384,512]{1,0:T(8,128)} %param.10, f32[384,512]{1,0:T(8,128)} %copy.42, f32[384]{0:T(512)S(1)} %add_rsqrt_fusion, f32[512]{0:T(512)} %param.11), kind=kLoop, calls=%fused_computation.54 | loop fusion | flops 1178752 | bytes 1580032 | tf_op jit(solution)/shard_map/reduce_sum | solution.py:83
  89.3 5.6 %psum.22 = f32[384]{0:T(512)} all-reduce(f32[384]{0:T(512)} %get-tuple-element.13), channel_id=1, replica_groups=mesh['seq'=16,'head'=2] {'head'}, use_global_device_ids=true, to_apply=%region_3.4 | all-reduce | flops 384 | bytes 3072 | tf_op jit(solution)/shard_map/psum | solution.py:79
  94.9 0.7 fusion.74
  95.6 2.5 %multiply_subtract_fusion = f32[384,512]{1,0:T(8,128)} fusion(f32[384,512]{1,0:T(8,128)} %copy.42, f32[384,512]{1,0:T(8,128)} %param.10, f32[384]{0:T(512)S(1)} %fusion.74, f32[512]{0:T(512)} %param.11, f32[384]{0:T(512)} %copy-done.19), kind=kLoop, calls=%fused_computation.57 | loop fusion | flops 786432 | bytes 2364416 | tf_op jit(solution)/shard_map/sub | solution.py:82
  98.1 2.3 %copy.72 = f32[384,512]{0,1:T(8,128)} copy(f32[384,512]{1,0:T(8,128)} %multiply_subtract_fusion) | data formatting | bytes 1572864 | tf_op jit(solution)/shard_map/reshape | solution.py:85
  100.4 3.2 %fusion.60 = f32[4,128,128]{2,1,0:T(8,128)} fusion(f32[384,4,128]{0,2,1:T(8,128)} %bitcast.107, f32[384,4,128]{0,2,1:T(8,128)} %bitcast.112, f32[384,4]{0,1:T(4,128)} %get-tuple-element.25), kind=kOutput, calls=%fused_computation.55 | convolution fusion | flops 302186496 | bytes 1841152 | tf_op jit(solution)/shard_map/thd,the->hde/dot_general | solution.py:91
  104.2 0.5 maximum_convert_fusion
  104.8 0.6 broadcast.215.clone.1
  105.3 1.9 %convert_dynamic-update-slice_fusion = f32[16]{0:T(128)} fusion(f32[16]{0:T(128)} %broadcast.215.clone.1, u32[]{:T(128)} %bitcast.4, s32[384]{0:T(512)} %param.13), kind=kLoop, calls=%fused_computation.92 | loop fusion | flops 1 | bytes 1088
  107.2 30.7 %all-reduce.2 = (f32[16]{0:T(128)}, f32[512]{0:T(512)}) all-reduce(f32[16]{0:T(128)} %convert_dynamic-update-slice_fusion, f32[512]{0:T(512)} %get-tuple-element.12), channel_id=1, replica_groups=mesh['seq'=16,'head'=2] {'seq'}, use_global_device_ids=true, to_apply=%add.1 | all-reduce | flops 528 | bytes 4224
  138.0 4.0 %fusion.53 = f32[4,384,384]{2,1,0:T(8,128)S(1)} fusion(f32[384,4,128]{0,2,1:T(8,128)} %bitcast.108, f32[384,512]{1,0:T(8,128)S(1)} %copy-done), kind=kOutput, calls=%fused_computation.47 | convolution fusion | flops 905969664 | bytes 3932160 | tf_op jit(solution)/shard_map/ihe,jhe->hij/dot_general | solution.py:86
  142.0 3.1 %fusion.12 = f32[384,4,128]{0,2,1:T(8,128)S(1)} fusion(f32[384,4,128]{0,2,1:T(8,128)S(1)} %bitcast.116, f32[4,384,384]{2,1,0:T(8,128)S(1)} %fusion.53, f32[384,384]{1,0:T(8,128)S(1)} %copy-done.7, f32[4]{0:T(128)S(1)} %copy-done.21, pred[384,384]{1,0:T(8,128)(4,1)S(1)} %fusion.71), kind=kOutput, calls=%fused_computation.10 | convolution fusion | flops 907739136 | bytes 4669456 | tf_op jit(solution)/shard_map/hij,jhd->ihd/dot_general | solution.py:87
  145.1 1.6 fusion.34
  146.7 1.9 %copy.56 = bf16[384,512]{1,0:T(8,128)(2,1)} copy(bf16[384,512]{0,1:T(8,128)(2,1)} %bitcast.122) | data formatting | bytes 786432
  148.6 0.8 compare_and_fusion
  149.4 1.2 select_bitcast_fusion
  150.5 4.7 %fusion.21 = f32[384,4,128]{0,2,1:T(8,128)} fusion(f32[384,4,128]{0,2,1:T(8,128)} %bitcast.109, f32[4,384,384]{2,1,0:T(8,128)S(1)} %fusion.58, f32[384,384]{1,0:T(8,128)} %copy-done.6, f32[4]{0:T(128)} %copy-done.20, pred[384,384]{1,0:T(8,128)(4,1)S(1)} %fusion.71), kind=kOutput, calls=%fused_computation.13 | convolution fusion | flops 907739136 | bytes 4669456 | tf_op jit(solution)/shard_map/hij,ihe->jhe/dot_general | solution.py:105
  155.3 2.6 %fusion.15 = f32[384,4,128]{0,2,1:T(8,128)S(1)} fusion(f32[384,4,128]{0,2,1:T(8,128)S(1)} %bitcast.114, f32[4,384,384]{2,1,0:T(8,128)S(1)} %copy-done.2, f32[384,384]{1,0:T(8,128)S(1)} %copy-done.8, f32[4]{0:T(128)S(1)} %copy-done.22, pred[384,384]{1,0:T(8,128)(4,1)S(1)} %fusion.71), kind=kOutput, calls=%fused_computation.11 | convolution fusion | flops 907739136 | bytes 4669456 | tf_op jit(solution)/shard_map/hij,ihd->jhd/dot_general | solution.py:101
  158.0 2.9 %multiply_reduce_fusion = f32[4,128,128]{2,1,0:T(8,128)S(1)} fusion(f32[4,16,128,128]{3,2,0,1:T(8,128)} %bitcast.118, f32[4,16]{0,1:T(8,128)S(1)} %select_bitcast_fusion), kind=kLoop, calls=%fused_computation | loop fusion | flops 2031616 | bytes 4456704 | tf_op jit(solution)/shard_map/nh,nhde->hde/dot_general | solution.py:44
  160.9 1.8 %fusion.32 = bf16[384,4,128]{0,2,1:T(8,128)(2,1)} fusion(f32[384,4,128]{0,2,1:T(8,128)S(1)} %copy-done.12, f32[4,128,128]{2,1,0:T(8,128)S(1)} %multiply_reduce_fusion, f32[384,4]{0,1:T(4,128)S(1)} %copy-done.15, f32[384,512]{1,0:T(8,128)S(1)} %copy-done.11), kind=kOutput, calls=%fused_computation.26 | convolution fusion | flops 302579712 | bytes 2234368 | tf_op jit(solution)/shard_map/jhd,hde->jhe/dot_general | solution.py:106
  162.7 1.9 %copy.58 = bf16[384,512]{1,0:T(8,128)(2,1)} copy(bf16[384,512]{0,1:T(8,128)(2,1)} %bitcast.124) | data formatting | bytes 786432
  164.6 1.1 fusion.33
  165.7 0.9 copy.57
  (57 shorter events, 0.2 us)
Async XLA Ops:
  7.2 6.3 %copy-start = (f32[384,512]{1,0:T(8,128)S(1)}, f32[384,512]{1,0:T(8,128)}, u32[]{:S(2)}) copy-start(f32[384,512]{1,0:T(8,128)} %param.9) | copy-start | bytes 2359300
  7.2 8.0 %copy-start.24 = (u32[32]{0:T(128)S(1)}, u32[32]{0:T(128)}, u32[]{:S(2)}) copy-start(u32[32]{0:T(128)} %constant.31) | copy-start | bytes 388
  7.2 8.5 %copy-start.18 = (s32[384]{0:T(512)S(1)}, s32[384]{0:T(512)}, u32[]{:S(2)}) copy-start(s32[384]{0:T(512)} %param.13) | copy-start | bytes 4612
  7.2 46.1 %copy-start.14 = (f32[384,512]{1,0:T(8,128)S(1)}, f32[384,512]{1,0:T(8,128)}, u32[]{:S(2)}) copy-start(f32[384,512]{1,0:T(8,128)} %param.7) | copy-start | bytes 2359300
  7.2 61.5 %all-gather.5.cloned.1.call-start = ((), (), s32[]{:S(2)}) async-start(), calls=%async_computation | async-start | bytes 4456448 | tf_op jit(solution)/shard_map/all_gather | solution.py:64
  8.0 46.4 %copy-start.23 = (f32[4]{0:T(128)}, f32[4]{0:T(128)S(1)}, u32[]{:S(2)}) copy-start(f32[4]{0:T(128)S(1)} %get-tuple-element.26) | copy-start | bytes 52
  8.0 50.8 %copy-start.20 = (f32[4]{0:T(128)}, f32[4]{0:T(128)S(1)}, u32[]{:S(2)}) copy-start(f32[4]{0:T(128)S(1)} %get-tuple-element.27) | copy-start | bytes 52
  10.8 44.0 %copy-start.9 = (f32[384,512]{0,1:T(8,128)}, f32[384,512]{0,1:T(8,128)S(1)}, u32[]{:S(2)}) copy-start(f32[384,512]{0,1:T(8,128)S(1)} %copy.101) | copy-start | bytes 2359300
  15.1 142.9 %all-gather.7.cloned.1.call-start = ((), (), s32[]{:S(2)}) async-start(), calls=%async_computation.1 | async-start | bytes 4456448 | tf_op jit(solution)/shard_map/all_gather | solution.py:95
  54.6 4.3 %copy-start.6 = (f32[384,384]{1,0:T(8,128)}, f32[384,384]{1,0:T(8,128)S(1)}, u32[]{:S(2)}) copy-start(f32[384,384]{1,0:T(8,128)S(1)} %fusion.69) | copy-start | bytes 1769476
  68.7 6.6 %copy-start.4 = (f32[384,512]{0,1:T(8,128)S(1)}, f32[384,512]{0,1:T(8,128)}, u32[]{:S(2)}) copy-start(f32[384,512]{0,1:T(8,128)} %copy.71) | copy-start | bytes 2359300
  68.7 6.6 %copy-start.13 = (f32[384,4,128]{0,2,1:T(8,128)S(1)}, f32[384,4,128]{0,2,1:T(8,128)}, u32[]{:S(2)}) copy-start(f32[384,4,128]{0,2,1:T(8,128)} %fusion.18) | copy-start | bytes 2359300
  68.7 6.6 %copy-start.16 = (f32[384,4]{0,1:T(4,128)S(1)}, f32[384,4]{0,1:T(4,128)}, u32[]{:S(2)}) copy-start(f32[384,4]{0,1:T(4,128)} %get-tuple-element.24) | copy-start | bytes 18436
  86.5 0.6 copy-start.19
  137.9 4.0 %copy-start.7 = (f32[384,384]{1,0:T(8,128)S(1)}, f32[384,384]{1,0:T(8,128)}, u32[]{:S(2)}) copy-start(f32[384,384]{1,0:T(8,128)} %copy-done.6) | copy-start | bytes 1769476
  138.0 4.0 %copy-start.10 = (f32[384,512]{0,1:T(8,128)S(1)}, f32[384,512]{0,1:T(8,128)}, u32[]{:S(2)}) copy-start(f32[384,512]{0,1:T(8,128)} %copy-done.9) | copy-start | bytes 2359300
  138.0 4.0 %copy-start.21 = (f32[4]{0:T(128)S(1)}, f32[4]{0:T(128)}, u32[]{:S(2)}) copy-start(f32[4]{0:T(128)} %copy-done.20) | copy-start | bytes 52
  141.9 4.7 %copy-start.1 = (f32[4,384,384]{2,1,0:T(8,128)}, f32[4,384,384]{2,1,0:T(8,128)S(1)}, u32[]{:S(2)}) copy-start(f32[4,384,384]{2,1,0:T(8,128)S(1)} %fusion.53) | copy-start | bytes 7077892
  142.0 3.1 %copy-start.3 = (f32[384,512]{0,1:T(8,128)S(1)}, f32[384,512]{0,1:T(8,128)}, u32[]{:S(2)}) copy-start(f32[384,512]{0,1:T(8,128)} %copy.72) | copy-start | bytes 2359300
  142.0 3.1 %copy-start.17 = (f32[384,4]{0,1:T(4,128)S(1)}, f32[384,4]{0,1:T(4,128)}, u32[]{:S(2)}) copy-start(f32[384,4]{0,1:T(4,128)} %get-tuple-element.24) | copy-start | bytes 18436
  148.6 6.7 %copy-start.2 = (f32[4,384,384]{2,1,0:T(8,128)S(1)}, f32[4,384,384]{2,1,0:T(8,128)}, u32[]{:S(2)}) copy-start(f32[4,384,384]{2,1,0:T(8,128)} %copy-done.1) | copy-start | bytes 7077892
  148.6 6.7 %copy-start.5 = (f32[384,512]{0,1:T(8,128)S(1)}, f32[384,512]{0,1:T(8,128)}, u32[]{:S(2)}) copy-start(f32[384,512]{0,1:T(8,128)} %copy.71) | copy-start | bytes 2359300
  148.6 6.7 %copy-start.8 = (f32[384,384]{1,0:T(8,128)S(1)}, f32[384,384]{1,0:T(8,128)}, u32[]{:S(2)}) copy-start(f32[384,384]{1,0:T(8,128)} %copy-done.6) | copy-start | bytes 1769476
  148.6 6.7 %copy-start.22 = (f32[4]{0:T(128)S(1)}, f32[4]{0:T(128)}, u32[]{:S(2)}) copy-start(f32[4]{0:T(128)} %copy-done.20) | copy-start | bytes 52
  157.9 3.0 %copy-start.11 = (f32[384,512]{1,0:T(8,128)S(1)}, f32[384,512]{1,0:T(8,128)}, u32[]{:S(2)}) copy-start(f32[384,512]{1,0:T(8,128)} %param.8) | copy-start | bytes 2359300
  157.9 3.0 %copy-start.12 = (f32[384,4,128]{0,2,1:T(8,128)S(1)}, f32[384,4,128]{0,2,1:T(8,128)}, u32[]{:S(2)}) copy-start(f32[384,4,128]{0,2,1:T(8,128)} %fusion.21) | copy-start | bytes 2359300
  158.0 3.0 %copy-start.15 = (f32[384,4]{0,1:T(4,128)S(1)}, f32[384,4]{0,1:T(4,128)}, u32[]{:S(2)}) copy-start(f32[384,4]{0,1:T(4,128)} %get-tuple-element.16) | copy-start | bytes 18436
Sparse Core Ops, SparseCore 0:
  15.2 53.4 all-gather.4
  103.7 49.1 all-gather.6
where the time goes:
time: 174 us; the launch traced here: 173 us
  blocking collectives  77.5 us (45%)
  matrix products  40.7 us (23%)
  other arithmetic  17.8 us (10%)
  local copies, waits for them, and re-layouts  15.8 us (9%)
  between operations  15.7 us (9%)
  waiting for transfers between devices  5.9 us (3%)
    unnamed x2, blocking collectives  66.1 us
    psum x2, blocking collectives, body(): squares, product = lax.psum((square_part, product_part), 'head')  11.4 us
    unnamed x56, local copies, waits for them, and re-layouts  6.59 us
    dot_general x1, matrix products, weighted_carry(): return jnp.einsum('nh,nhde->hde', factor, states_all, precision=PRECISE)  6.55 us
    all_gather x1, waiting for transfers between devices, body(): lax.all_gather(state_loc[None], 'seq', axis=0, tiled=True)  5.84 us
    dot_general x1, matrix products, body(): jnp.einsum('hij,ihe->jhe', scores, grad_heads, precision=PRECISE)  4.75 us
    dot_general x1, matrix products, body(): jnp.einsum('ihd,jhd->hij', query_rows, key_rows, precision=PRECISE)  4.05 us
    dot_general x1, matrix products, body(): outputs = jnp.einsum('hij,jhd->ihd', scores, value_rows, precision=PRECISE)  3.97 us
  transfers between devices with their start and end apart: 2, of which 1 were waited for; matrix products, arithmetic and copies ran while one was open for 20% of the time, Pallas kernels for 0%

commit v1 on v0

v1 whole, which is shorter than its diff:
```python
import functools

import jax
import jax.numpy as jnp
from jax import lax
from jax.experimental import pallas as pl
from jax.experimental.pallas import tpu as pltpu
from jax.sharding import PartitionSpec as P

HEAD_DIM = 128
PAD = HEAD_DIM + 8
EPSILON = 1e-06
F32 = jnp.float32
BF16 = jnp.bfloat16


def split(x):
    hi = x.astype(BF16)
    return hi, (x - hi.astype(F32)).astype(BF16)


def dot(a, b, ca, cb):
    return lax.dot_general(a, b, (((ca,), (cb,)), ((), ())), preferred_element_type=F32)


def cat(parts, axis=1):
    return jnp.concatenate(parts, axis=axis)


def rows_by_rows(a, b):
    return dot(cat([a[0], a[1], a[0]]), cat([b[0], b[0], b[1]]), 1, 1)


def fold(both):
    return both[:, :HEAD_DIM] + both[:, HEAD_DIM:]


def square_by_rows(a, b):
    half = cat([b[0], b[1]])
    return fold(dot(cat(list(a)), cat([half, half], 0), 1, 0))


def square_by_cols(a, b):
    half = cat([b[0], b[1]], 0)
    return fold(dot(cat(list(a)), cat([half, half]), 1, 1))


def tokens_outer(a, b):
    both = fold(dot(cat(list(a)), cat(list(b)), 0, 0))
    return both[:HEAD_DIM] + both[HEAD_DIM:]


def kernel(
    shape, q_hbm, k_hbm, v_hbm, g_hbm, gain_ref, rates, seg_ref,
    qg_ref, kg_ref, vg_ref, gain_out,
    q, k, v, g, w, a_hi, a_lo, p_hi, p_lo, out, grad, cols,
    loc, inbox, gsend, ginbox, csend, carry,
    hsend, hinbox, nsend, ninbox, tsend, tinbox,
    in_sem, st_s, st_r, gr_s, gr_r, ca_s, ca_r, hd_s, hd_r, ng_s, ng_r, nt_s, nt_r,
):
    heads, length, n_seq, n_head, groups, reach = shape
    me = lax.axis_index("seq")
    hx = lax.axis_index("head")
    pos = lax.rem(me, heads)
    z = lax.div(me, heads)
    base = z * heads
    features = float(heads * HEAD_DIM * n_head)

    def load(i, h):
        src, dst = ((k_hbm, k), (v_hbm, v), (q_hbm, q), (g_hbm, g))[i]
        return pltpu.make_async_copy(
            src.at[:, pl.ds(h * HEAD_DIM, HEAD_DIM)], dst.at[h], in_sem.at[i, h]
        )

    for i, h in [(0, h) for h in range(heads)] + [(1, h) for h in range(heads)]:
        load(i, h).start()
    for i in (2, 3):
        for h in range(heads):
            load(i, h).start()

    def remote(src, dst, ss, rs, **where):
        return pltpu.make_async_remote_copy(
            src_ref=src, dst_ref=dst, send_sem=ss, recv_sem=rs,
            device_id=where, device_id_type=pl.DeviceIdType.MESH,
        )

    barrier = pltpu.get_barrier_semaphore()

    def greet(**where):
        pl.semaphore_signal(barrier, inc=1, device_id=where, device_id_type=pl.DeviceIdType.MESH)

    for o in range(1, heads):
        greet(seq=base + lax.rem(pos + o, heads))
    for o in range(1, groups):
        greet(seq=lax.rem(z + o, groups) * heads + pos)
    for o in range(1, n_head):
        greet(head=lax.rem(hx + o, n_head))

    seg_row = seg_ref[...].astype(F32)
    first = seg_row[0:1, 0:1]
    last = seg_row[0:1, length - 1 : length]
    seg_col = jnp.broadcast_to(seg_row, (HEAD_DIM, length)).T
    place = lax.broadcasted_iota(jnp.int32, (length, HEAD_DIM), 0).astype(F32)
    head_first = jnp.where(seg_col == first, 1.0, 0.0)
    tail_last = jnp.where(seg_col == last, 1.0, 0.0)
    for h in range(heads):
        rate = rates[h]
        cols[0, h] = jnp.exp(-rate * (place + 1.0)) * head_first
        cols[1, h] = jnp.exp(-rate * (length - place)) * tail_last

    def send_states(t):
        for h in range(heads):
            @pl.when(h != pos)
            def _(h=h):
                remote(loc.at[t, h], inbox.at[t, pos], st_s.at[t, h], st_r.at[t, pos], seq=base + h).start()

    row_id = lax.broadcasted_iota(jnp.int32, (8, HEAD_DIM), 0)
    meta = jnp.where(row_id == 0, last, jnp.where(row_id == 1, first, 0.0))
    for h in range(heads):
        load(0, h).wait()
        load(1, h).wait()
        out_w = jnp.exp(-rates[h] * (length - 1.0 - place)) * tail_last
        loc[0, h, :HEAD_DIM] = tokens_outer(split(k[h] * out_w), split(v[h]))
        loc[0, h, HEAD_DIM:] = meta
    pl.semaphore_wait(barrier, (heads - 1) + (groups - 1) + (n_head - 1))
    send_states(0)

    def weigh(h):
        rate = rates[h]
        row_w = lax.broadcasted_iota(jnp.int32, (length, length), 0)
        col_w = lax.broadcasted_iota(jnp.int32, (length, length), 1)
        gap = (row_w - col_w).astype(F32)
        same = cat([seg_col] * (length // HEAD_DIM)) == seg_row
        w[h] = jnp.where((gap >= 0.0) & same, jnp.exp(-rate * jnp.maximum(gap, 0.0)), 0.0)

    def score(h):
        hi, lo = split(rows_by_rows(split(q[h]), split(k[h])) * w[h])
        a_hi[h] = hi
        a_lo[h] = lo

    def mix(h):
        hi, lo = split(rows_by_rows(split(grad[h]), split(v[h])) * w[h])
        p_hi[h] = hi
        p_lo[h] = lo

    def by_rows(hi, lo, b):
        return fold(dot(hi, cat(list(b)), 1, 0)) + dot(lo, b[0], 1, 0)

    def by_cols(hi, lo, b):
        return fold(dot(hi, cat(list(b)), 0, 0)) + dot(lo, b[0], 0, 0)

    own_step = jnp.exp(jnp.broadcast_to(-rates[pos] * float(length), (1, HEAD_DIM)))
    own_group = jnp.exp(jnp.broadcast_to(-rates[pos] * float(length * heads), (1, HEAD_DIM)))

    def on_group(t, d, action):
        there = z + d if t == 0 else z - d
        ok = there < groups if t == 0 else there >= 0

        @pl.when(ok)
        def _():
            action(remote(
                gsend.at[t], ginbox.at[t, d - 1], gr_s.at[t, d - 1], gr_r.at[t, d - 1],
                seq=there * heads + pos,
            ))

    def gather_group(t):
        inbox[t, pos] = loc[t, pos]
        for p in range(heads):
            @pl.when(p != pos)
            def _(p=p):
                remote(loc.at[t, p], inbox.at[t, p], st_s.at[t, p], st_r.at[t, p], seq=base + p).wait_recv()
        order = list(range(heads)) if t == 0 else list(range(heads))[::-1]
        near, far = (HEAD_DIM, HEAD_DIM + 1) if t == 0 else (HEAD_DIM + 1, HEAD_DIM)
        total = None
        for i, p in enumerate(order):
            state = inbox[t, p, :HEAD_DIM]
            if i > 0:
                before = order[i - 1]
                keep = inbox[t, before, near : near + 1] == inbox[t, p, far : far + 1]
                came = jnp.where(keep, total, 0.0)
                csend[t, p] = came
                through = inbox[t, p, near : near + 1] == inbox[t, p, far : far + 1]
                total = state + jnp.where(through, own_step, 0.0) * came
            else:
                total = state
        gsend[t, :HEAD_DIM] = total
        gsend[t, HEAD_DIM:] = jnp.broadcast_to(inbox[t, order[-1], near : near + 1], (8, HEAD_DIM))
        for d in range(1, reach + 1):
            on_group(t, d, lambda c: c.start())

    def carry_out(t):
        order = list(range(heads)) if t == 0 else list(range(heads))[::-1]
        near, far = (HEAD_DIM, HEAD_DIM + 1) if t == 0 else (HEAD_DIM + 1, HEAD_DIM)
        for d in range(1, reach + 1):
            there = z - d if t == 0 else z + d
            ok = there >= 0 if t == 0 else there < groups

            @pl.when(ok)
            def _(d=d):
                remote(
                    gsend.at[t], ginbox.at[t, d - 1], gr_s.at[t, d - 1], gr_r.at[t, d - 1], seq=me
                ).wait_recv()

            @pl.when(jnp.logical_not(ok))
            def _(d=d):
                ginbox[t, d - 1] = jnp.full((PAD, HEAD_DIM), -1.0, F32)
        enter = jnp.zeros((HEAD_DIM, HEAD_DIM), F32)
        factor = jnp.ones((1, HEAD_DIM), F32)
        for d in range(1, reach + 1):
            keep = ginbox[t, d - 1, HEAD_DIM : HEAD_DIM + 1] == inbox[t, order[0], far : far + 1]
            enter = enter + jnp.where(keep, factor, 0.0) * ginbox[t, d - 1, :HEAD_DIM]
            factor = factor * own_group
        factor = jnp.ones((1, HEAD_DIM), F32)
        for i, p in enumerate(order):
            if i == 0:
                csend[t, p] = enter
            else:
                before = order[i - 1]
                through = (
                    (inbox[t, before, near : near + 1] == inbox[t, p, far : far + 1])
                    & (inbox[t, before, near : near + 1] == inbox[t, before, far : far + 1])
                )
                factor = factor * jnp.where(through, own_step, 0.0)
                csend[t, p] = csend[t, p] + factor * enter
        for p in range(heads):
            @pl.when(p != pos)
            def _(p=p):
                remote(csend.at[t, p], carry.at[t, pos], ca_s.at[t, p], ca_r.at[t, pos], seq=base + p).start()
        carry[t, pos] = csend[t, pos]

    def wait_carry(t):
        for h in range(heads):
            @pl.when(h != pos)
            def _(h=h):
                remote(csend.at[t, h], carry.at[t, h], ca_s.at[t, h], ca_r.at[t, h], seq=base + h).wait_recv()

    for h in range(heads):
        weigh(h)
    for h in range(heads):
        load(2, h).wait()
    gather_group(0)
    for h in range(heads):
        score(h)
    carry_out(0)
    for h in range(heads):
        out[h] = by_rows(a_hi[h], a_lo[h], split(v[h]))
    for h in range(heads):
        load(3, h).wait()
    wait_carry(0)
    squares = jnp.zeros((length, HEAD_DIM), F32)
    product = jnp.zeros((length, HEAD_DIM), F32)
    for h in range(heads):
        o = out[h] + cols[0, h] * square_by_rows(split(q[h]), split(carry[0, h]))
        out[h] = o
        shaped = g[h] * gain_ref[:, h * HEAD_DIM : (h + 1) * HEAD_DIM]
        grad[h] = shaped
        squares = squares + o * o
        product = product + shaped * o
    sums = cat([
        jnp.sum(squares.T, axis=0, keepdims=True),
        jnp.sum(product.T, axis=0, keepdims=True),
        jnp.zeros((6, length), F32),
    ], 0)
    hsend[...] = sums
    for o in range(1, n_head):
        other = lax.rem(hx + o, n_head)
        remote(hsend, hinbox.at[hx], hd_s.at[o], hd_r.at[hx], head=other).start()
    hinbox[hx] = sums
    for o in range(1, n_head):
        other = lax.rem(hx + o, n_head)
        remote(hsend, hinbox.at[other], hd_s.at[o], hd_r.at[other], head=other).wait_recv()
    sums = hinbox[0]
    for i in range(1, n_head):
        sums = sums + hinbox[i]
    inv_row = lax.rsqrt(sums[0:1] / features + EPSILON)
    coef_row = inv_row * inv_row * inv_row * (sums[1:2] / features)
    inv = jnp.broadcast_to(inv_row, (HEAD_DIM, length)).T
    coef = jnp.broadcast_to(coef_row, (HEAD_DIM, length)).T
    for h in range(heads):
        o = out[h]
        d_out = inv * grad[h] - coef * o
        grad[h] = d_out
        back_w = jnp.exp(-rates[h] * place) * head_first
        loc[1, h, :HEAD_DIM] = tokens_outer(split(q[h] * back_w), split(d_out))
        part = jnp.sum(g[h] * o * inv, axis=0, keepdims=True)
        loc[1, h, HEAD_DIM:] = jnp.where(row_id == 2, part, meta)
    send_states(1)

    for h in range(heads):
        mix(h)
    gather_group(1)
    part = inbox[1, 0, HEAD_DIM:]
    for p in range(1, heads):
        part = part + inbox[1, p, HEAD_DIM:]
    nsend[...] = part
    ninbox[z] = part
    for o in range(1, groups):
        other = lax.rem(z + o, groups)
        remote(nsend, ninbox.at[z], ng_s.at[o], ng_r.at[z], seq=other * heads + pos).start()
    for h in range(heads):
        lanes = pl.ds(h * HEAD_DIM, HEAD_DIM)
        part = by_rows(p_hi[h], p_lo[h], split(k[h]))
        part = part + cols[0, h] * square_by_cols(split(grad[h]), split(carry[0, h]))
        qg_ref[:, lanes] = part.astype(BF16)
    carry_out(1)
    for h in range(heads):
        out[h] = by_cols(p_hi[h], p_lo[h], split(q[h]))
        g[h] = by_cols(a_hi[h], a_lo[h], split(grad[h]))
    for o in range(1, groups):
        other = lax.rem(z + o, groups)
        remote(nsend, ninbox.at[other], ng_s.at[o], ng_r.at[other], seq=me).wait_recv()
    part = ninbox[0]
    for i in range(1, groups):
        part = part + ninbox[i]
    tsend[...] = part
    tinbox[pos] = part
    for p in range(heads):
        @pl.when(p != pos)
        def _(p=p):
            remote(tsend, tinbox.at[pos], nt_s.at[p], nt_r.at[pos], seq=base + p).start()
    wait_carry(1)
    for h in range(heads):
        lanes = pl.ds(h * HEAD_DIM, HEAD_DIM)
        state = split(carry[1, h])
        kg_ref[:, lanes] = (out[h] + cols[1, h] * square_by_cols(split(v[h]), state)).astype(BF16)
        vg_ref[:, lanes] = (g[h] + cols[1, h] * square_by_rows(split(k[h]), state)).astype(BF16)
    for p in range(heads):
        @pl.when(p != pos)
        def _(p=p):
            remote(tsend, tinbox.at[p], nt_s.at[p], nt_r.at[p], seq=base + p).wait_recv()
    for h in range(heads):
        gain_out[:, h * HEAD_DIM : (h + 1) * HEAD_DIM] = tinbox[h, 2:3]

    for t in range(2):
        for h in range(heads):
            @pl.when(h != pos)
            def _(t=t, h=h):
                remote(loc.at[t, h], inbox.at[t, pos], st_s.at[t, h], st_r.at[t, pos], seq=base + h).wait_send()
                remote(csend.at[t, h], carry.at[t, pos], ca_s.at[t, h], ca_r.at[t, pos], seq=base + h).wait_send()
        for d in range(1, reach + 1):
            on_group(t, d, lambda c: c.wait_send())
    for o in range(1, n_head):
        remote(hsend, hinbox.at[hx], hd_s.at[o], hd_r.at[hx], head=lax.rem(hx + o, n_head)).wait_send()
    for o in range(1, groups):
        other = lax.rem(z + o, groups)
        remote(nsend, ninbox.at[z], ng_s.at[o], ng_r.at[z], seq=other * heads + pos).wait_send()
    for p in range(heads):
        @pl.when(p != pos)
        def _(p=p):
            remote(tsend, tinbox.at[pos], nt_s.at[p], nt_r.at[pos], seq=base + p).wait_send()


def body(n_seq, n_head, queries, key_vectors, value_vectors, out_grad, norm_gain, decay_rates, segment_ids):
    length, width = queries.shape
    heads = width // HEAD_DIM
    groups = n_seq // heads
    longest = (length * n_seq) // 3
    blocks = -(-(longest - 1) // length)
    reach = min(-(-blocks // heads), groups - 1)
    shape = (heads, length, n_seq, n_head, groups, reach)
    any_spec = pl.BlockSpec(memory_space=pl.ANY)
    vmem = pl.BlockSpec(memory_space=pltpu.VMEM)
    tok = (heads, length, HEAD_DIM)
    sq = (heads, length, length)
    dma = pltpu.SemaphoreType.DMA
    outs = pl.pallas_call(
        functools.partial(kernel, shape),
        out_shape=(
            jax.ShapeDtypeStruct((length, width), BF16),
            jax.ShapeDtypeStruct((length, width), BF16),
            jax.ShapeDtypeStruct((length, width), BF16),
            jax.ShapeDtypeStruct((1, width), F32),
        ),
        in_specs=[any_spec] * 4 + [vmem, pl.BlockSpec(memory_space=pltpu.SMEM), vmem],
        out_specs=(vmem,) * 4,
        scratch_shapes=[
            pltpu.VMEM(tok, F32), pltpu.VMEM(tok, F32), pltpu.VMEM(tok, F32), pltpu.VMEM(tok, F32),
            pltpu.VMEM(sq, F32),
            pltpu.VMEM(sq, BF16), pltpu.VMEM(sq, BF16), pltpu.VMEM(sq, BF16), pltpu.VMEM(sq, BF16),
            pltpu.VMEM(tok, F32), pltpu.VMEM(tok, F32),
            pltpu.VMEM((2,) + tok, F32),
            pltpu.VMEM((2, heads, PAD, HEAD_DIM), F32),
            pltpu.VMEM((2, heads, PAD, HEAD_DIM), F32),
            pltpu.VMEM((2, PAD, HEAD_DIM), F32),
            pltpu.VMEM((2, reach, PAD, HEAD_DIM), F32),
            pltpu.VMEM((2, heads, HEAD_DIM, HEAD_DIM), F32),
            pltpu.VMEM((2, heads, HEAD_DIM, HEAD_DIM), F32),
            pltpu.VMEM((8, length), F32),
            pltpu.VMEM((n_head, 8, length), F32),
            pltpu.VMEM((8, HEAD_DIM), F32),
            pltpu.VMEM((groups, 8, HEAD_DIM), F32),
            pltpu.VMEM((8, HEAD_DIM), F32),
            pltpu.VMEM((heads, 8, HEAD_DIM), F32),
            dma((4, heads)),
            dma((2, heads)), dma((2, heads)),
            dma((2, reach)), dma((2, reach)),
            dma((2, heads)), dma((2, heads)),
            dma((n_head,)), dma((n_head,)),
            dma((groups,)), dma((groups,)),
            dma((heads,)), dma((heads,)),
        ],
        compiler_params=pltpu.CompilerParams(
            collective_id=0, has_side_effects=True, vmem_limit_bytes=40 * 1024 * 1024
        ),
        name="decayed_attention_grad",
    )(
        queries, key_vectors, value_vectors, out_grad,
        norm_gain.reshape(1, width), decay_rates, segment_ids.reshape(1, length),
    )
    return outs[0], outs[1], outs[2], outs[3].reshape(width)


def solution(mesh):
    return jax.shard_map(
        functools.partial(body, mesh.shape["seq"], mesh.shape["head"]),
        mesh=mesh,
        in_specs=(
            P("seq", "head"),
            P("seq", "head"),
            P("seq", "head"),
            P("seq", "head"),
            P("head"),
            P("head"),
            P("seq"),
        ),
        out_specs=(P("seq", "head"), P("seq", "head"), P("seq", "head"), P("head")),
        check_vma=False,
    )
```

time: 174 us -> 48.7 us (0.28)
  blocking collectives: 77.5 us -> 0 us
  matrix products: 40.7 us -> 0 us
  Pallas kernels: 0 us -> 39.6 us
  other arithmetic: 17.8 us -> 0 us
  between operations: 15.7 us -> 0.67 us
  local copies, waits for them, and re-layouts: 15.8 us -> 8.05 us
  waiting for transfers between devices: 5.9 us -> 0 us
    unnamed x2 -> x0, blocking collectives: 66.1 us -> none
    dot_general x13 -> x0, matrix products: 40.7 us -> none  [the longest x1 6.55 us: weighted_carry(): return jnp.einsum('nh,nhde->hde', factor, states_all, precision=PRECISE)]
    pallas_call x0 -> x1, Pallas kernels: none -> 39.6 us  [body(): pl.pallas_call(functools.partial(kernel, shape), out_shape=(jax.ShapeDtyp...]
    psum x2 -> x0, blocking collectives: 11.4 us -> none  [body(): squares, product = lax.psum((square_part, product_part), 'head')]
    reshape x4 -> x1, local copies, waits for them, and re-layouts: 7.16 us -> 0.7 us  [body(): segment_ids.reshape(1, length)]
    all_gather x2 -> x0, waiting for transfers between devices: 5.87 us -> none  [the longest x1 5.84 us: body(): lax.all_gather(state_loc[None], 'seq', axis=0, tiled=True)]
    unnamed x3 -> x0, other arithmetic: 3.75 us -> none
    dot_general x1 -> x0, other arithmetic: 2.88 us -> none  [weighted_carry(): return jnp.einsum('nh,nhde->hde', factor, states_all, precision=PRECISE)]
  transfers between devices with their start and end apart: 2 -> 0, of which waited for: 1 -> 0; matrix products, arithmetic and copies ran while one was open for 20% -> 0% of each run, Pallas kernels for 0% -> 0%
where the time goes in v1:
time: 48.7 us; the launch traced here: 48.3 us
  Pallas kernels  39.6 us (81%)
  local copies, waits for them, and re-layouts  8.05 us (17%)
  between operations  0.67 us (1%)
    pallas_call x1, Pallas kernels, body(): pl.pallas_call(functools.partial(kernel, shape), out_shape=(jax.ShapeDtyp...  39.6 us
    unnamed x16, local copies, waits for them, and re-layouts  7.35 us

profile of v1, /device:TPU:0, one launch (start us, length us, event | category | flops | bytes accessed | tf_op | source)
XLA Modules:
  0.0 48.3 jit_solution(1751812394777586108)
XLA Ops:
  0.6 0.0 copy-start.4
  0.6 0.0 copy-start.5
  0.7 0.7 %reshape.18.seg_ref = s32[1,384]{1,0:T(1,128)S(1)} reshape(s32[384]{0:T(512)} %param.13) | data formatting | bytes 3072 | tf_op jit(solution)/shard_map/reshape | solution.py:408
  1.3 0.0 copy-done.4
  1.3 0.0 copy-done.5
  1.4 0.0 copy-start
  1.4 1.1 %copy-done = f32[384,512]{1,0:T(8,128)S(1)} copy-done((f32[384,512]{1,0:T(8,128)S(1)}, f32[384,512]{1,0:T(8,128)}, u32[]{:S(2)}) %copy-start) | copy-done | bytes 786456
  2.5 0.0 copy-start.1
  2.5 1.1 %copy-done.1 = f32[384,512]{1,0:T(8,128)S(1)} copy-done((f32[384,512]{1,0:T(8,128)S(1)}, f32[384,512]{1,0:T(8,128)}, u32[]{:S(2)}) %copy-start.1) | copy-done | bytes 786456
  3.6 0.0 copy-start.2
  3.6 1.1 %copy-done.2 = f32[384,512]{1,0:T(8,128)S(1)} copy-done((f32[384,512]{1,0:T(8,128)S(1)}, f32[384,512]{1,0:T(8,128)}, u32[]{:S(2)}) %copy-start.2) | copy-done | bytes 786456
  4.8 0.0 copy-start.3
  4.8 1.1 %copy-done.3 = f32[384,512]{1,0:T(8,128)S(1)} copy-done((f32[384,512]{1,0:T(8,128)S(1)}, f32[384,512]{1,0:T(8,128)}, u32[]{:S(2)}) %copy-start.3) | copy-done | bytes 786456
  5.9 39.6 %decayed_attention_grad.1 = (bf16[384,512]{1,0:T(8,128)(2,1)S(1)}, bf16[384,512]{1,0:T(8,128)(2,1)S(1)}, bf16[384,512]{1,0:T(8,128)(2,1)S(1)}, f32[1,512]{1,0:T(1,128)S(1)}) custom-call(f32[384,512]{1,0:T(8,128)S(1)} %copy-done, f32[384,512]{1,0:T(8,128)S(1)} %copy-done.1, f32[384,512]{1,0:T(8,128)S(1)} %copy-done.2, f32[384,512]{1,0:T(8,128)S(1)} %copy-done.3, ...), custom_call_target="tpu_custom_call" | custom-call | tf_op jit(solution)/shard_map/decayed_attention_grad/pallas_call | solution.py:366
  45.5 0.7 %copy.15 = bf16[384,512]{1,0:T(8,128)(2,1)} copy(bf16[384,512]{1,0:T(8,128)(2,1)S(1)} %get-tuple-element.16) | data formatting | bytes 786432
  46.3 0.7 %copy.16 = bf16[384,512]{1,0:T(8,128)(2,1)} copy(bf16[384,512]{1,0:T(8,128)(2,1)S(1)} %get-tuple-element.17) | data formatting | bytes 786432
  47.0 0.7 %copy.17 = bf16[384,512]{1,0:T(8,128)(2,1)} copy(bf16[384,512]{1,0:T(8,128)(2,1)S(1)} %get-tuple-element.18) | data formatting | bytes 786432
  47.8 0.6 %copy.18 = f32[512]{0:T(512)} copy(f32[512]{0:T(512)S(1)} %bitcast.3) | data formatting | bytes 4096
Async XLA Ops:
  0.6 0.7 %copy-start.4 = (f32[512]{0:T(512)S(1)}, f32[512]{0:T(512)}, u32[]{:S(2)}) copy-start(f32[512]{0:T(512)} %param.11) | copy-start | bytes 6148
  0.6 0.7 %copy-start.5 = (f32[4]{0:T(128)S(1)}, f32[4]{0:T(128)}, u32[]{:S(2)}) copy-start(f32[4]{0:T(128)} %rates.1) | copy-start | bytes 52
  1.4 1.1 %copy-start = (f32[384,512]{1,0:T(8,128)S(1)}, f32[384,512]{1,0:T(8,128)}, u32[]{:S(2)}) copy-start(f32[384,512]{1,0:T(8,128)} %q_hbm.1) | copy-start | bytes 2359300
  2.5 1.1 %copy-start.1 = (f32[384,512]{1,0:T(8,128)S(1)}, f32[384,512]{1,0:T(8,128)}, u32[]{:S(2)}) copy-start(f32[384,512]{1,0:T(8,128)} %k_hbm.1) | copy-start | bytes 2359300
  3.6 1.1 %copy-start.2 = (f32[384,512]{1,0:T(8,128)S(1)}, f32[384,512]{1,0:T(8,128)}, u32[]{:S(2)}) copy-start(f32[384,512]{1,0:T(8,128)} %v_hbm.1) | copy-start | bytes 2359300
  4.8 1.1 %copy-start.3 = (f32[384,512]{1,0:T(8,128)S(1)}, f32[384,512]{1,0:T(8,128)}, u32[]{:S(2)}) copy-start(f32[384,512]{1,0:T(8,128)} %g_hbm.1) | copy-start | bytes 2359300

commit v2 on v1

v2 whole, which is shorter than its diff:
```python
import functools

import jax
import jax.numpy as jnp
from jax import lax
from jax.experimental import pallas as pl
from jax.experimental.pallas import tpu as pltpu
from jax.sharding import PartitionSpec as P

HEAD_DIM = 128
CHUNKS = 2
ROWS = HEAD_DIM // CHUNKS
PAD = ROWS + 8
CORES = 2
VMEM_BYTES = 63 * 1024 * 1024
EPSILON = 1e-06
F32 = jnp.float32
BF16 = jnp.bfloat16


def split(x):
    hi = x.astype(BF16)
    return hi, (x - hi.astype(F32)).astype(BF16)


def dot(a, b, ca, cb):
    return lax.dot_general(a, b, (((ca,), (cb,)), ((), ())), preferred_element_type=F32)


def cat(parts, axis=1):
    return jnp.concatenate(parts, axis=axis)


def rows_by_rows(a, b):
    return dot(cat([a[0], a[1], a[0]]), cat([b[0], b[0], b[1]]), 1, 1)


def fold(both):
    return both[:, :HEAD_DIM] + both[:, HEAD_DIM:]


def square_by_rows(a, b):
    half = cat([b[0], b[1]])
    return fold(dot(cat(list(a)), cat([half, half], 0), 1, 0))


def square_by_cols(a, b):
    half = cat([b[0], b[1]], 0)
    return fold(dot(cat(list(a)), cat([half, half]), 1, 1))


def turned(x):
    return cat(list(split(x.T)), 0)


def outer(a_t, b):
    both = fold(dot(a_t, cat(list(split(b))), 1, 0))
    return both[:HEAD_DIM] + both[HEAD_DIM:]


def under(a_t, hi, lo):
    both = dot(a_t, hi, 1, 0)
    return (both[:HEAD_DIM] + both[HEAD_DIM:] + dot(a_t[:HEAD_DIM], lo, 1, 0)).T


def kernel(
    shape, q_hbm, k_hbm, v_hbm, g_hbm, gain_ref, rates, seg_ref,
    qg_ref, kg_ref, vg_ref, gain_out,
    q, k, v, g, w, a_hi, a_lo, p_hi, p_lo, out, grad, cols, q_t,
    loc, inbox, gsend, ginbox, csend, carry,
    hsend, hinbox, nsend, ninbox, tsend, tinbox,
    in_sem, st_s, st_r, gr_s, gr_r, ca_s, ca_r, hd_s, hd_r, ng_s, ng_r, nt_s, nt_r,
):
    heads, length, n_seq, n_head, groups, reach = shape
    me = lax.axis_index("seq")
    hx = lax.axis_index("head")
    pos = lax.rem(me, heads)
    z = lax.div(me, heads)
    base = z * heads
    features = float(heads * HEAD_DIM * n_head)

    def load(i, h):
        src, dst = ((k_hbm, k), (v_hbm, v), (q_hbm, q), (g_hbm, g))[i]
        return pltpu.make_async_copy(
            src.at[:, pl.ds(h * HEAD_DIM, HEAD_DIM)], dst.at[h], in_sem.at[i, h]
        )

    for i, h in [(0, h) for h in range(heads)] + [(1, h) for h in range(heads)]:
        load(i, h).start()
    for i in (2, 3):
        for h in range(heads):
            load(i, h).start()

    def remote(src, dst, ss, rs, **where):
        return pltpu.make_async_remote_copy(
            src_ref=src, dst_ref=dst, send_sem=ss, recv_sem=rs,
            device_id=where, device_id_type=pl.DeviceIdType.MESH,
        )

    barrier = pltpu.get_barrier_semaphore()

    def greet(**where):
        pl.semaphore_signal(barrier, inc=1, device_id=where, device_id_type=pl.DeviceIdType.MESH)

    for o in range(1, heads):
        greet(seq=base + lax.rem(pos + o, heads))
    for o in range(1, groups):
        greet(seq=lax.rem(z + o, groups) * heads + pos)
    for o in range(1, n_head):
        greet(head=lax.rem(hx + o, n_head))

    seg_row = seg_ref[...].reshape(1, length).astype(F32)
    first = seg_row[0:1, 0:1]
    last = seg_row[0:1, length - 1 : length]
    seg_col = jnp.broadcast_to(seg_row, (HEAD_DIM, length)).T
    place = lax.broadcasted_iota(jnp.int32, (length, HEAD_DIM), 0).astype(F32)
    head_first = jnp.where(seg_col == first, 1.0, 0.0)
    tail_last = jnp.where(seg_col == last, 1.0, 0.0)
    for h in range(heads):
        rate = rates[h]
        cols[0, h] = jnp.exp(-rate * (place + 1.0)) * head_first
        cols[1, h] = jnp.exp(-rate * (length - place)) * tail_last

    side = lax.div(pos, CORES)
    sides = heads // CORES

    def post(t, members):
        for c in range(CHUNKS):
            for m in members:
                remote(
                    loc.at[t, m, c], inbox.at[t, pos, c], st_s.at[t, m, c], st_r.at[t, pos, c], seq=base + m
                ).start()

    def put(t, m, state, tail):
        for c in range(CHUNKS):
            loc[t, m, c, :ROWS] = state[c * ROWS : (c + 1) * ROWS]
            loc[t, m, c, ROWS:] = tail

    def others(o):
        there = lax.rem(side + o, sides) * CORES
        return [there + i for i in range(CORES)]

    mates = [side * CORES + lax.rem(pos - side * CORES + i, CORES) for i in range(1, CORES)]
    rounds = [others(o) for o in range(1, sides)] + [mates]

    row_id = lax.broadcasted_iota(jnp.int32, (8, HEAD_DIM), 0)
    meta = jnp.where(row_id == 0, last, jnp.where(row_id == 1, first, 0.0))

    def local_state(m):
        out_w = jnp.exp(-rates[m] * (length - 1.0 - place)) * tail_last
        put(0, m, outer(turned(k[m]), v[m] * out_w), meta)

    for h in range(heads):
        load(0, h).wait()
        load(1, h).wait()
    for i, members in enumerate(rounds):
        for m in members:
            local_state(m)
        if i == 0:
            pl.semaphore_wait(barrier, (heads - 1) + (groups - 1) + (n_head - 1))
        post(0, members)
    local_state(pos)

    def weigh(h):
        rate = rates[h]
        row_w = lax.broadcasted_iota(jnp.int32, (length, length), 0)
        col_w = lax.broadcasted_iota(jnp.int32, (length, length), 1)
        gap = (row_w - col_w).astype(F32)
        same = cat([seg_col] * (length // HEAD_DIM)) == seg_row
        w[h] = jnp.where((gap >= 0.0) & same, jnp.exp(-rate * jnp.maximum(gap, 0.0)), 0.0)

    def score(h):
        hi, lo = split(rows_by_rows(split(q[h]), split(k[h])) * w[h])
        a_hi[h] = hi
        a_lo[h] = lo

    def mix(h):
        hi, lo = split(rows_by_rows(split(grad[h]), split(v[h])) * w[h])
        p_hi[h] = hi
        p_lo[h] = lo

    def by_rows(hi, lo, b):
        return fold(dot(hi, cat(list(b)), 1, 0)) + dot(lo, b[0], 1, 0)

    own_step = jnp.exp(jnp.broadcast_to(-rates[pos] * float(length), (1, HEAD_DIM)))
    own_group = jnp.exp(jnp.broadcast_to(-rates[pos] * float(length * heads), (1, HEAD_DIM)))

    def on_group(t, d, c, action):
        there = z + d if t == 0 else z - d
        ok = there < groups if t == 0 else there >= 0

        @pl.when(ok)
        def _():
            action(remote(
                gsend.at[t, c], ginbox.at[t, d - 1, c], gr_s.at[t, d - 1, c], gr_r.at[t, d - 1, c],
                seq=there * heads + pos,
            ))

    def direction(t):
        order = list(range(heads))
        return (order, ROWS, ROWS + 1) if t == 0 else (order[::-1], ROWS + 1, ROWS)

    def gather_group(t, c):
        inbox[t, pos, c] = loc[t, pos, c]
        for p in range(heads):
            @pl.when(p != pos)
            def _(p=p):
                remote(
                    loc.at[t, p, c], inbox.at[t, p, c], st_s.at[t, p, c], st_r.at[t, p, c], seq=base + p
                ).wait_recv()
        order, near, far = direction(t)
        total = None
        for i, p in enumerate(order):
            state = inbox[t, p, c, :ROWS]
            if i > 0:
                before = order[i - 1]
                keep = inbox[t, before, c, near : near + 1] == inbox[t, p, c, far : far + 1]
                came = jnp.where(keep, total, 0.0)
                csend[t, p, c] = came
                through = inbox[t, p, c, near : near + 1] == inbox[t, p, c, far : far + 1]
                total = state + jnp.where(through, own_step, 0.0) * came
            else:
                total = state
        gsend[t, c, :ROWS] = total
        gsend[t, c, ROWS:] = jnp.broadcast_to(inbox[t, order[-1], c, near : near + 1], (8, HEAD_DIM))
        for d in range(1, reach + 1):
            on_group(t, d, c, lambda copy: copy.start())

    def carry_out(t, c):
        order, near, far = direction(t)
        for d in range(1, reach + 1):
            there = z - d if t == 0 else z + d
            ok = there >= 0 if t == 0 else there < groups

            @pl.when(ok)
            def _(d=d):
                remote(
                    gsend.at[t, c], ginbox.at[t, d - 1, c], gr_s.at[t, d - 1, c], gr_r.at[t, d - 1, c],
                    seq=lax.rem(me + heads, n_seq),
                ).wait_recv()

            @pl.when(jnp.logical_not(ok))
            def _(d=d):
                ginbox[t, d - 1, c] = jnp.full((PAD, HEAD_DIM), -1.0, F32)
        enter = jnp.zeros((ROWS, HEAD_DIM), F32)
        factor = jnp.ones((1, HEAD_DIM), F32)
        for d in range(1, reach + 1):
            keep = ginbox[t, d - 1, c, ROWS : ROWS + 1] == inbox[t, order[0], c, far : far + 1]
            enter = enter + jnp.where(keep, factor, 0.0) * ginbox[t, d - 1, c, :ROWS]
            factor = factor * own_group
        factor = jnp.ones((1, HEAD_DIM), F32)
        for i, p in enumerate(order):
            if i == 0:
                csend[t, p, c] = enter
            else:
                before = order[i - 1]
                through = (
                    (inbox[t, before, c, near : near + 1] == inbox[t, p, c, far : far + 1])
                    & (inbox[t, before, c, near : near + 1] == inbox[t, before, c, far : far + 1])
                )
                factor = factor * jnp.where(through, own_step, 0.0)
                csend[t, p, c] = csend[t, p, c] + factor * enter
        for m in [m for members in rounds for m in members]:
            remote(
                csend.at[t, m, c], carry.at[t, pos, c], ca_s.at[t, m, c], ca_r.at[t, pos, c], seq=base + m
            ).start()
        carry[t, pos, c] = csend[t, pos, c]

    def wait_carry(t):
        for c in range(CHUNKS):
            for m in [m for members in rounds for m in members]:
                remote(
                    csend.at[t, m, c], carry.at[t, m, c], ca_s.at[t, m, c], ca_r.at[t, m, c], seq=base + m
                ).wait_recv()

    def carried(t, h):
        return split(carry[t, h].reshape(HEAD_DIM, HEAD_DIM))

    def weave(work, steps, lead):
        rest = max(len(work) - lead, 1)
        done = 0
        for i, piece in enumerate(work):
            piece()
            due = (i + 1 - lead) * len(steps) // rest if i + 1 > lead else 0
            while done < min(due, len(steps)):
                steps[done]()
                done += 1
        while done < len(steps):
            steps[done]()
            done += 1

    def turn(h):
        q_t[h] = turned(q[h])

    def intra(h):
        out[h] = by_rows(a_hi[h], a_lo[h], split(v[h]))

    def each(f):
        return [functools.partial(f, h) for h in range(heads)]

    def chunks(f, t):
        return [functools.partial(f, t, c) for c in range(CHUNKS)]

    for h in range(heads):
        weigh(h)
    for h in range(heads):
        load(2, h).wait()
    weave(each(score) + each(turn) + each(intra), chunks(gather_group, 0) + chunks(carry_out, 0), 1)
    for h in range(heads):
        load(3, h).wait()
    wait_carry(0)
    squares = jnp.zeros((length, HEAD_DIM), F32)
    product = jnp.zeros((length, HEAD_DIM), F32)
    for h in range(heads):
        o = out[h] + cols[0, h] * square_by_rows(split(q[h]), carried(0, h))
        out[h] = o
        shaped = g[h] * gain_ref[:, h * HEAD_DIM : (h + 1) * HEAD_DIM]
        grad[h] = shaped
        squares = squares + o * o
        product = product + shaped * o
    sums = cat([
        jnp.sum(squares.T, axis=0, keepdims=True),
        jnp.sum(product.T, axis=0, keepdims=True),
        jnp.zeros((6, length), F32),
    ], 0)
    hsend[...] = sums
    for o in range(1, n_head):
        other = lax.rem(hx + o, n_head)
        remote(hsend, hinbox.at[hx], hd_s.at[o], hd_r.at[hx], head=other).start()
    hinbox[hx] = sums
    for o in range(1, n_head):
        other = lax.rem(hx + o, n_head)
        remote(hsend, hinbox.at[other], hd_s.at[o], hd_r.at[other], head=other).wait_recv()
    sums = hinbox[0]
    for i in range(1, n_head):
        sums = sums + hinbox[i]
    inv_row = lax.rsqrt(sums[0:1] / features + EPSILON)
    coef_row = inv_row * inv_row * inv_row * (sums[1:2] / features)
    inv = jnp.broadcast_to(inv_row, (HEAD_DIM, length)).T
    coef = jnp.broadcast_to(coef_row, (HEAD_DIM, length)).T

    def local_back(m):
        o = out[m]
        d_out = inv * grad[m] - coef * o
        grad[m] = d_out
        back_w = jnp.exp(-rates[m] * place) * head_first
        part = jnp.sum(g[m] * o * inv, axis=0, keepdims=True)
        put(1, m, outer(q_t[m], d_out * back_w), jnp.where(row_id == 2, part, meta))

    for members in rounds:
        for m in members:
            local_back(m)
        post(1, members)
    local_back(pos)

    def group_gain():
        part = inbox[1, 0, 0, ROWS:]
        for p in range(1, heads):
            part = part + inbox[1, p, 0, ROWS:]
        nsend[...] = part
        ninbox[z] = part
        for o in range(1, groups):
            other = lax.rem(z + o, groups)
            remote(nsend, ninbox.at[z], ng_s.at[o], ng_r.at[z], seq=other * heads + pos).start()

    def whole_gain():
        for o in range(1, groups):
            other = lax.rem(z + o, groups)
            remote(nsend, ninbox.at[other], ng_s.at[o], ng_r.at[other], seq=other * heads + pos).wait_recv()
        part = ninbox[0]
        for i in range(1, groups):
            part = part + ninbox[i]
        tsend[...] = part
        tinbox[pos] = part
        for p in range(heads):
            @pl.when(p != pos)
            def _(p=p):
                remote(tsend, tinbox.at[pos], nt_s.at[p], nt_r.at[pos], seq=base + p).start()

    def for_queries(h):
        lanes = pl.ds(h * HEAD_DIM, HEAD_DIM)
        part = by_rows(p_hi[h], p_lo[h], split(k[h]))
        part = part + cols[0, h] * square_by_cols(split(grad[h]), carried(0, h))
        qg_ref[:, lanes] = part.astype(BF16)

    def for_keys(h):
        out[h] = under(q_t[h], p_hi[h], p_lo[h])

    def for_values(h):
        g[h] = under(turned(grad[h]), a_hi[h], a_lo[h])

    steps = chunks(gather_group, 1) + [group_gain] + chunks(carry_out, 1) + [whole_gain]
    weave(each(mix) + each(for_queries) + each(for_keys) + each(for_values), steps, heads)
    wait_carry(1)
    for h in range(heads):
        lanes = pl.ds(h * HEAD_DIM, HEAD_DIM)
        state = carried(1, h)
        kg_ref[:, lanes] = (out[h] + cols[1, h] * square_by_cols(split(v[h]), state)).astype(BF16)
        vg_ref[:, lanes] = (g[h] + cols[1, h] * square_by_rows(split(k[h]), state)).astype(BF16)
    for p in range(heads):
        @pl.when(p != pos)
        def _(p=p):
            remote(tsend, tinbox.at[p], nt_s.at[p], nt_r.at[p], seq=base + p).wait_recv()
    for h in range(heads):
        gain_out[:, h * HEAD_DIM : (h + 1) * HEAD_DIM] = tinbox[h, 2:3]

    for t in range(2):
        for c in range(CHUNKS):
            for m in [m for members in rounds for m in members]:
                remote(
                    loc.at[t, m, c], inbox.at[t, pos, c], st_s.at[t, m, c], st_r.at[t, pos, c], seq=base + m
                ).wait_send()
                remote(
                    csend.at[t, m, c], carry.at[t, pos, c], ca_s.at[t, m, c], ca_r.at[t, pos, c], seq=base + m
                ).wait_send()
            for d in range(1, reach + 1):
                on_group(t, d, c, lambda copy: copy.wait_send())
    for o in range(1, n_head):
        remote(hsend, hinbox.at[hx], hd_s.at[o], hd_r.at[hx], head=lax.rem(hx + o, n_head)).wait_send()
    for o in range(1, groups):
        other = lax.rem(z + o, groups)
        remote(nsend, ninbox.at[z], ng_s.at[o], ng_r.at[z], seq=other * heads + pos).wait_send()
    for p in range(heads):
        @pl.when(p != pos)
        def _(p=p):
            remote(tsend, tinbox.at[pos], nt_s.at[p], nt_r.at[pos], seq=base + p).wait_send()


def store(*refs):
    sem = refs[-1]
    copies = [pltpu.make_async_copy(refs[i], refs[4 + i], sem.at[i]) for i in range(4)]
    for copy in copies:
        copy.start()
    for copy in copies:
        copy.wait()


def body(n_seq, n_head, queries, key_vectors, value_vectors, out_grad, norm_gain, decay_rates, segment_ids):
    length, width = queries.shape
    heads = width // HEAD_DIM
    groups = n_seq // heads
    longest = (length * n_seq) // 3
    blocks = -(-(longest - 1) // length)
    reach = min(-(-blocks // heads), groups - 1)
    shape = (heads, length, n_seq, n_head, groups, reach)
    any_spec = pl.BlockSpec(memory_space=pl.ANY)
    vmem = pl.BlockSpec(memory_space=pltpu.VMEM)
    tok = (heads, length, HEAD_DIM)
    sq = (heads, length, length)
    dma = pltpu.SemaphoreType.DMA
    outs = pl.pallas_call(
        functools.partial(kernel, shape),
        out_shape=(
            jax.ShapeDtypeStruct((length, width), BF16),
            jax.ShapeDtypeStruct((length, width), BF16),
            jax.ShapeDtypeStruct((length, width), BF16),
            jax.ShapeDtypeStruct((1, width), F32),
        ),
        in_specs=[any_spec] * 4 + [vmem, pl.BlockSpec(memory_space=pltpu.SMEM), vmem],
        out_specs=(vmem,) * 4,
        scratch_shapes=[
            pltpu.VMEM(tok, F32), pltpu.VMEM(tok, F32), pltpu.VMEM(tok, F32), pltpu.VMEM(tok, F32),
            pltpu.VMEM(sq, F32),
            pltpu.VMEM(sq, BF16), pltpu.VMEM(sq, BF16), pltpu.VMEM(sq, BF16), pltpu.VMEM(sq, BF16),
            pltpu.VMEM(tok, F32), pltpu.VMEM(tok, F32),
            pltpu.VMEM((2,) + tok, F32),
            pltpu.VMEM((heads, 2 * HEAD_DIM, length), BF16),
            pltpu.VMEM((2, heads, CHUNKS, PAD, HEAD_DIM), F32),
            pltpu.VMEM((2, heads, CHUNKS, PAD, HEAD_DIM), F32),
            pltpu.VMEM((2, CHUNKS, PAD, HEAD_DIM), F32),
            pltpu.VMEM((2, reach, CHUNKS, PAD, HEAD_DIM), F32),
            pltpu.VMEM((2, heads, CHUNKS, ROWS, HEAD_DIM), F32),
            pltpu.VMEM((2, heads, CHUNKS, ROWS, HEAD_DIM), F32),
            pltpu.VMEM((8, length), F32),
            pltpu.VMEM((n_head, 8, length), F32),
            pltpu.VMEM((8, HEAD_DIM), F32),
            pltpu.VMEM((groups, 8, HEAD_DIM), F32),
            pltpu.VMEM((8, HEAD_DIM), F32),
            pltpu.VMEM((heads, 8, HEAD_DIM), F32),
            dma((4, heads)),
            dma((2, heads, CHUNKS)), dma((2, heads, CHUNKS)),
            dma((2, reach, CHUNKS)), dma((2, reach, CHUNKS)),
            dma((2, heads, CHUNKS)), dma((2, heads, CHUNKS)),
            dma((n_head,)), dma((n_head,)),
            dma((groups,)), dma((groups,)),
            dma((heads,)), dma((heads,)),
        ],
        compiler_params=pltpu.CompilerParams(
            collective_id=0, has_side_effects=True, vmem_limit_bytes=VMEM_BYTES
        ),
        name="decayed_attention_grad",
    )(
        queries, key_vectors, value_vectors, out_grad,
        norm_gain.reshape(1, width), decay_rates, segment_ids,
    )
    outs = pl.pallas_call(
        store,
        out_shape=tuple(jax.ShapeDtypeStruct(x.shape, x.dtype) for x in outs),
        in_specs=[any_spec] * 4,
        out_specs=(any_spec,) * 4,
        scratch_shapes=[dma((4,))],
        compiler_params=pltpu.CompilerParams(vmem_limit_bytes=VMEM_BYTES),
        name="store_results",
    )(*outs)
    return outs[0], outs[1], outs[2], outs[3].reshape(width)


def solution(mesh):
    return jax.shard_map(
        functools.partial(body, mesh.shape["seq"], mesh.shape["head"]),
        mesh=mesh,
        in_specs=(
            P("seq", "head"),
            P("seq", "head"),
            P("seq", "head"),
            P("seq", "head"),
            P("head"),
            P("head"),
            P("seq"),
        ),
        out_specs=(P("seq", "head"), P("seq", "head"), P("seq", "head"), P("head")),
        check_vma=False,
    )
```

time: 48.7 us -> 76.3 us (1.57)
  Pallas kernels: 39.6 us -> 75.5 us
  local copies, waits for them, and re-layouts: 8.05 us -> 0 us
    pallas_call x0 -> x1, Pallas kernels: none -> 36.9 us  [body(): pl.pallas_call(store, out_shape=tuple((jax.ShapeDtypeStruct(x.shape, x.dt...]
    unnamed x16 -> x0, local copies, waits for them, and re-layouts: 7.35 us -> none
    pallas_call x1, Pallas kernels: 39.6 us -> 38.6 us  [body(): pl.pallas_call(functools.partial(kernel, shape), out_shape=(jax.ShapeDtyp...]
where the time goes in v2:
time: 76.3 us; the launch traced here: 76.1 us
  Pallas kernels  75.5 us (99%)
    pallas_call x1, Pallas kernels, body(): pl.pallas_call(functools.partial(kernel, shape), out_shape=(jax.ShapeDtyp...  38.6 us
    pallas_call x1, Pallas kernels, body(): pl.pallas_call(store, out_shape=tuple((jax.ShapeDtypeStruct(x.shape, x.dt...  36.9 us

profile of v2, /device:TPU:0, one launch (start us, length us, event | category | flops | bytes accessed | tf_op | source)
XLA Modules:
  0.0 76.1 jit_solution(12872795400294893177)
XLA Ops:
  0.6 38.6 %decayed_attention_grad.1 = (bf16[384,512]{1,0:T(8,128)(2,1)}, bf16[384,512]{1,0:T(8,128)(2,1)}, bf16[384,512]{1,0:T(8,128)(2,1)}, f32[1,512]{1,0:T(1,128)}) custom-call(f32[384,512]{1,0:T(8,128)} %q_hbm.1, f32[384,512]{1,0:T(8,128)} %k_hbm.1, f32[384,512]{1,0:T(8,128)} %v_hbm.1, f32[384,512]{1,0:T(8,128)} %g_hbm.1, f32[1,512]{1,0:T(1,128)} %bitcast.2, ...), custom_call_target="tpu_custom_call" | custom-call | tf_op jit(solution)/shard_map/decayed_attention_grad/pallas_call | solution.py:451
  39.2 36.9 %store_results.1 = (bf16[384,512]{1,0:T(8,128)(2,1)}, bf16[384,512]{1,0:T(8,128)(2,1)}, bf16[384,512]{1,0:T(8,128)(2,1)}, f32[1,512]{1,0:T(1,128)}) custom-call(bf16[384,512]{1,0:T(8,128)(2,1)} %get-tuple-element.12.refs_0_, bf16[384,512]{1,0:T(8,128)(2,1)} %get-tuple-element.13.refs_1_, bf16[384,512]{1,0:T(8,128)(2,1)} %get-tuple-element.14.refs_2_, ...), custom_call_target="tpu_custom_call" | custom-call | tf_op jit(solution)/shard_map/store_results/pallas_call | solution.py:496

commit v3 on v2

--- a/solution.py
+++ b/solution.py
@@ -79,17 +79,32 @@
     base = z * heads
     features = float(heads * HEAD_DIM * n_head)
 
+    def lanes_of(h):
+        return pl.ds(pl.multiple_of(h * HEAD_DIM, HEAD_DIM), HEAD_DIM)
+
     def load(i, h):
         src, dst = ((k_hbm, k), (v_hbm, v), (q_hbm, q), (g_hbm, g))[i]
         return pltpu.make_async_copy(
-            src.at[:, pl.ds(h * HEAD_DIM, HEAD_DIM)], dst.at[h], in_sem.at[i, h]
+            src.at[:, lanes_of(h)], dst.at[h], in_sem.at[i, h]
         )
 
-    for i, h in [(0, h) for h in range(heads)] + [(1, h) for h in range(heads)]:
-        load(i, h).start()
+    side = lax.div(pos, CORES)
+    sides = heads // CORES
+
+    def others(o):
+        there = lax.rem(side + o, sides) * CORES
+        return [there + i for i in range(CORES)]
+
+    mates = [side * CORES + lax.rem(pos - side * CORES + i, CORES) for i in range(1, CORES)]
+    rounds = [others(o) for o in range(1, sides)] + [mates]
+    peers = [m for members in rounds for m in members]
+
+    for m in peers + [pos]:
+        load(0, m).start()
+        load(1, m).start()
     for i in (2, 3):
-        for h in range(heads):
-            load(i, h).start()
+        for m in range(heads):
+            load(i, m).start()
 
     def remote(src, dst, ss, rs, **where):
         return pltpu.make_async_remote_copy(
@@ -121,9 +136,6 @@
         cols[0, h] = jnp.exp(-rate * (place + 1.0)) * head_first
         cols[1, h] = jnp.exp(-rate * (length - place)) * tail_last
 
-    side = lax.div(pos, CORES)
-    sides = heads // CORES
-
     def post(t, members):
         for c in range(CHUNKS):
             for m in members:
@@ -136,23 +148,15 @@
             loc[t, m, c, :ROWS] = state[c * ROWS : (c + 1) * ROWS]
             loc[t, m, c, ROWS:] = tail
 
-    def others(o):
-        there = lax.rem(side + o, sides) * CORES
-        return [there + i for i in range(CORES)]
-
-    mates = [side * CORES + lax.rem(pos - side * CORES + i, CORES) for i in range(1, CORES)]
-    rounds = [others(o) for o in range(1, sides)] + [mates]
-
     row_id = lax.broadcasted_iota(jnp.int32, (8, HEAD_DIM), 0)
     meta = jnp.where(row_id == 0, last, jnp.where(row_id == 1, first, 0.0))
 
     def local_state(m):
+        load(0, m).wait()
+        load(1, m).wait()
         out_w = jnp.exp(-rates[m] * (length - 1.0 - place)) * tail_last
         put(0, m, outer(turned(k[m]), v[m] * out_w), meta)
 
-    for h in range(heads):
-        load(0, h).wait()
-        load(1, h).wait()
     for i, members in enumerate(rounds):
         for m in members:
             local_state(m)
@@ -260,18 +264,17 @@
                 )
                 factor = factor * jnp.where(through, own_step, 0.0)
                 csend[t, p, c] = csend[t, p, c] + factor * enter
-        for m in [m for members in rounds for m in members]:
+        for m in peers:
             remote(
                 csend.at[t, m, c], carry.at[t, pos, c], ca_s.at[t, m, c], ca_r.at[t, pos, c], seq=base + m
             ).start()
         carry[t, pos, c] = csend[t, pos, c]
 
-    def wait_carry(t):
+    def wait_carry(t, m):
         for c in range(CHUNKS):
-            for m in [m for members in rounds for m in members]:
-                remote(
-                    csend.at[t, m, c], carry.at[t, m, c], ca_s.at[t, m, c], ca_r.at[t, m, c], seq=base + m
-                ).wait_recv()
+            remote(
+                csend.at[t, m, c], carry.at[t, m, c], ca_s.at[t, m, c], ca_r.at[t, m, c], seq=base + m
+            ).wait_recv()
 
     def carried(t, h):
         return split(carry[t, h].reshape(HEAD_DIM, HEAD_DIM))
@@ -308,16 +311,20 @@
     weave(each(score) + each(turn) + each(intra), chunks(gather_group, 0) + chunks(carry_out, 0), 1)
     for h in range(heads):
         load(3, h).wait()
-    wait_carry(0)
+    def shape_grad(h):
+        grad[h] = g[h] * gain_ref[:, lanes_of(h)]
+
+    for h in range(heads):
+        shape_grad(h)
     squares = jnp.zeros((length, HEAD_DIM), F32)
     product = jnp.zeros((length, HEAD_DIM), F32)
-    for h in range(heads):
-        o = out[h] + cols[0, h] * square_by_rows(split(q[h]), carried(0, h))
-        out[h] = o
-        shaped = g[h] * gain_ref[:, h * HEAD_DIM : (h + 1) * HEAD_DIM]
-        grad[h] = shaped
+    for m in [pos] + peers[::-1]:
+        if m is not pos:
+            wait_carry(0, m)
+        o = out[m] + cols[0, m] * square_by_rows(split(q[m]), carried(0, m))
+        out[m] = o
         squares = squares + o * o
-        product = product + shaped * o
+        product = product + grad[m] * o
     sums = cat([
         jnp.sum(squares.T, axis=0, keepdims=True),
         jnp.sum(product.T, axis=0, keepdims=True),
@@ -391,12 +398,12 @@
 
     steps = chunks(gather_group, 1) + [group_gain] + chunks(carry_out, 1) + [whole_gain]
     weave(each(mix) + each(for_queries) + each(for_keys) + each(for_values), steps, heads)
-    wait_carry(1)
-    for h in range(heads):
-        lanes = pl.ds(h * HEAD_DIM, HEAD_DIM)
-        state = carried(1, h)
-        kg_ref[:, lanes] = (out[h] + cols[1, h] * square_by_cols(split(v[h]), state)).astype(BF16)
-        vg_ref[:, lanes] = (g[h] + cols[1, h] * square_by_rows(split(k[h]), state)).astype(BF16)
+    for m in [pos] + peers[::-1]:
+        if m is not pos:
+            wait_carry(1, m)
+        state = carried(1, m)
+        kg_ref[:, lanes_of(m)] = (out[m] + cols[1, m] * square_by_cols(split(v[m]), state)).astype(BF16)
+        vg_ref[:, lanes_of(m)] = (g[m] + cols[1, m] * square_by_rows(split(k[m]), state)).astype(BF16)
     for p in range(heads):
         @pl.when(p != pos)
         def _(p=p):
@@ -406,7 +413,7 @@
 
     for t in range(2):
         for c in range(CHUNKS):
-            for m in [m for members in rounds for m in members]:
+            for m in peers:
                 remote(
                     loc.at[t, m, c], inbox.at[t, pos, c], st_s.at[t, m, c], st_r.at[t, pos, c], seq=base + m
                 ).wait_send()
@@ -496,7 +503,7 @@
     outs = pl.pallas_call(
         store,
         out_shape=tuple(jax.ShapeDtypeStruct(x.shape, x.dtype) for x in outs),
-        in_specs=[any_spec] * 4,
+        in_specs=[vmem] * 4,
         out_specs=(any_spec,) * 4,
         scratch_shapes=[dma((4,))],
         compiler_params=pltpu.CompilerParams(vmem_limit_bytes=VMEM_BYTES),

time: 76.3 us -> 41.4 us (0.54)
  Pallas kernels: 75.5 us -> 40.6 us
    pallas_call x1, Pallas kernels: 36.9 us -> 2.28 us  [body(): pl.pallas_call(store, out_shape=tuple((jax.ShapeDtypeStruct(x.shape, x.dt...]
where the time goes in v3:
time: 41.4 us; the launch traced here: 41.3 us
  Pallas kernels  40.6 us (98%)
  between operations  0.64 us (2%)
    pallas_call x1, Pallas kernels, body(): pl.pallas_call(functools.partial(kernel, shape), out_shape=(jax.ShapeDtyp...  38.4 us
    pallas_call x1, Pallas kernels, body(): pl.pallas_call(store, out_shape=tuple((jax.ShapeDtypeStruct(x.shape, x.dt...  2.28 us

profile of v3, /device:TPU:0, one launch (start us, length us, event | category | flops | bytes accessed | tf_op | source)
XLA Modules:
  0.0 41.3 jit_solution(63689249764593716)
XLA Ops:
  0.6 38.4 %decayed_attention_grad.1 = (bf16[384,512]{1,0:T(8,128)(2,1)}, bf16[384,512]{1,0:T(8,128)(2,1)}, bf16[384,512]{1,0:T(8,128)(2,1)}, f32[1,512]{1,0:T(1,128)}) custom-call(f32[384,512]{1,0:T(8,128)} %q_hbm.1, f32[384,512]{1,0:T(8,128)} %k_hbm.1, f32[384,512]{1,0:T(8,128)} %v_hbm.1, f32[384,512]{1,0:T(8,128)} %g_hbm.1, f32[1,512]{1,0:T(1,128)} %bitcast.2, ...), custom_call_target="tpu_custom_call" | custom-call | tf_op jit(solution)/shard_map/decayed_attention_grad/pallas_call | solution.py:458
  39.0 2.3 %store_results.1 = (bf16[384,512]{1,0:T(8,128)(2,1)}, bf16[384,512]{1,0:T(8,128)(2,1)}, bf16[384,512]{1,0:T(8,128)(2,1)}, f32[1,512]{1,0:T(1,128)}) custom-call(bf16[384,512]{1,0:T(8,128)(2,1)} %get-tuple-element.12.refs_0_, bf16[384,512]{1,0:T(8,128)(2,1)} %get-tuple-element.13.refs_1_, bf16[384,512]{1,0:T(8,128)(2,1)} %get-tuple-element.14.refs_2_, ...), custom_call_target="tpu_custom_call" | custom-call | tf_op jit(solution)/shard_map/store_results/pallas_call | solution.py:503

commit v4 on v3

--- a/solution.py
+++ b/solution.py
@@ -12,6 +12,7 @@
 ROWS = HEAD_DIM // CHUNKS
 PAD = ROWS + 8
 CORES = 2
+GROUP = 256
 VMEM_BYTES = 63 * 1024 * 1024
 EPSILON = 1e-06
 F32 = jnp.float32
@@ -58,9 +59,35 @@
     return both[:HEAD_DIM] + both[HEAD_DIM:]
 
 
-def under(a_t, hi, lo):
-    both = dot(a_t, hi, 1, 0)
-    return (both[:HEAD_DIM] + both[HEAD_DIM:] + dot(a_t[:HEAD_DIM], lo, 1, 0)).T
+def column_groups(length):
+    return [(j, min(j + GROUP, length)) for j in range(0, length, GROUP)]
+
+
+def under(a_t, hi, lo, h):
+    length = hi.shape[1]
+    parts = []
+    for j, end in column_groups(length):
+        both = dot(a_t[:, j:], hi[h, j:, j:end], 1, 0)
+        part = both[:HEAD_DIM] + both[HEAD_DIM:] + dot(a_t[:HEAD_DIM, j:], lo[h, j:, j:end], 1, 0)
+        parts.append(part.T)
+    return cat(parts, 0)
+
+
+def by_rows(hi, lo, h, b):
+    length = hi.shape[1]
+    both = cat(list(b))
+    total = None
+    for j, end in column_groups(length):
+        part = fold(dot(hi[h, j:, j:end], both[j:end], 1, 0)) + dot(lo[h, j:, j:end], b[0][j:end], 1, 0)
+        total = part if total is None else cat([total[:j], total[j:] + part], 0)
+    return total
+
+
+def triangle(hi, lo, h, a, b, w):
+    length = hi.shape[1]
+    for j, end in column_groups(length):
+        part = rows_by_rows([x[j:] for x in a], [x[j:end] for x in b]) * w[h, j:, j:end]
+        hi[h, j:, j:end], lo[h, j:, j:end] = split(part)
 
 
 def kernel(
@@ -165,26 +192,35 @@
         post(0, members)
     local_state(pos)
 
+    cell_gap = (
+        lax.broadcasted_iota(jnp.int32, (HEAD_DIM, HEAD_DIM), 0)
+        - lax.broadcasted_iota(jnp.int32, (HEAD_DIM, HEAD_DIM), 1)
+    ).astype(F32)
+
     def weigh(h):
         rate = rates[h]
-        row_w = lax.broadcasted_iota(jnp.int32, (length, length), 0)
-        col_w = lax.broadcasted_iota(jnp.int32, (length, length), 1)
-        gap = (row_w - col_w).astype(F32)
-        same = cat([seg_col] * (length // HEAD_DIM)) == seg_row
-        w[h] = jnp.where((gap >= 0.0) & same, jnp.exp(-rate * jnp.maximum(gap, 0.0)), 0.0)
+        near_w = jnp.where(cell_gap >= 0.0, jnp.exp(-rate * jnp.maximum(cell_gap, 0.0)), 0.0)
+        far_w = jnp.exp(-rate * (cell_gap + float(HEAD_DIM)))
+        step = jnp.exp(jnp.broadcast_to(-rate * float(HEAD_DIM), (1, HEAD_DIM)))
+        factors = []
+        for _ in range(1, length // HEAD_DIM):
+            factors.append(far_w)
+            far_w = far_w * step
+        for j, end in column_groups(length):
+            for r in range(j, length, HEAD_DIM):
+                for c in range(j, end, HEAD_DIM):
+                    cell = jnp.zeros((HEAD_DIM, HEAD_DIM), F32)
+                    if r >= c:
+                        value = near_w if r == c else factors[(r - c) // HEAD_DIM - 1]
+                        same = seg_col[r : r + HEAD_DIM] == seg_row[:, c : c + HEAD_DIM]
+                        cell = jnp.where(same, value, 0.0)
+                    w[h, r : r + HEAD_DIM, c : c + HEAD_DIM] = cell
 
     def score(h):
-        hi, lo = split(rows_by_rows(split(q[h]), split(k[h])) * w[h])
-        a_hi[h] = hi
-        a_lo[h] = lo
+        triangle(a_hi, a_lo, h, split(q[h]), split(k[h]), w)
 
     def mix(h):
-        hi, lo = split(rows_by_rows(split(grad[h]), split(v[h])) * w[h])
-        p_hi[h] = hi
-        p_lo[h] = lo
-
-    def by_rows(hi, lo, b):
-        return fold(dot(hi, cat(list(b)), 1, 0)) + dot(lo, b[0], 1, 0)
+        triangle(p_hi, p_lo, h, split(grad[h]), split(v[h]), w)
 
     own_step = jnp.exp(jnp.broadcast_to(-rates[pos] * float(length), (1, HEAD_DIM)))
     own_group = jnp.exp(jnp.broadcast_to(-rates[pos] * float(length * heads), (1, HEAD_DIM)))
@@ -296,7 +332,7 @@
         q_t[h] = turned(q[h])
 
     def intra(h):
-        out[h] = by_rows(a_hi[h], a_lo[h], split(v[h]))
+        out[h] = by_rows(a_hi, a_lo, h, split(v[h]))
 
     def each(f):
         return [functools.partial(f, h) for h in range(heads)]
@@ -386,15 +422,15 @@
 
     def for_queries(h):
         lanes = pl.ds(h * HEAD_DIM, HEAD_DIM)
-        part = by_rows(p_hi[h], p_lo[h], split(k[h]))
+        part = by_rows(p_hi, p_lo, h, split(k[h]))
         part = part + cols[0, h] * square_by_cols(split(grad[h]), carried(0, h))
         qg_ref[:, lanes] = part.astype(BF16)
 
     def for_keys(h):
-        out[h] = under(q_t[h], p_hi[h], p_lo[h])
+        out[h] = under(q_t[h], p_hi, p_lo, h)
 
     def for_values(h):
-        g[h] = under(turned(grad[h]), a_hi[h], a_lo[h])
+        g[h] = under(turned(grad[h]), a_hi, a_lo, h)
 
     steps = chunks(gather_group, 1) + [group_gain] + chunks(carry_out, 1) + [whole_gain]
     weave(each(mix) + each(for_queries) + each(for_keys) + each(for_values), steps, heads)

time: 41.4 us -> 41.3 us (level)
  no operation moved by 1% of the time
where the time goes in v4:
time: 41.3 us; the launch traced here: 41.1 us
  Pallas kernels  40.5 us (98%)
  between operations  0.64 us (2%)
    pallas_call x1, Pallas kernels, body(): pl.pallas_call(functools.partial(kernel, shape), out_shape=(jax.ShapeDtyp...  38.2 us
    pallas_call x1, Pallas kernels, body(): pl.pallas_call(store, out_shape=tuple((jax.ShapeDtypeStruct(x.shape, x.dt...  2.28 us

profile of v4, /device:TPU:0, one launch (start us, length us, event | category | flops | bytes accessed | tf_op | source)
XLA Modules:
  0.0 41.1 jit_solution(13136575115013183838)
XLA Ops:
  0.6 38.2 %decayed_attention_grad.1 = (bf16[384,512]{1,0:T(8,128)(2,1)}, bf16[384,512]{1,0:T(8,128)(2,1)}, bf16[384,512]{1,0:T(8,128)(2,1)}, f32[1,512]{1,0:T(1,128)}) custom-call(f32[384,512]{1,0:T(8,128)} %q_hbm.1, f32[384,512]{1,0:T(8,128)} %k_hbm.1, f32[384,512]{1,0:T(8,128)} %v_hbm.1, f32[384,512]{1,0:T(8,128)} %g_hbm.1, f32[1,512]{1,0:T(1,128)} %bitcast.2, ...), custom_call_target="tpu_custom_call" | custom-call | tf_op jit(solution)/shard_map/decayed_attention_grad/pallas_call | solution.py:494
  38.8 2.3 %store_results.1 = (bf16[384,512]{1,0:T(8,128)(2,1)}, bf16[384,512]{1,0:T(8,128)(2,1)}, bf16[384,512]{1,0:T(8,128)(2,1)}, f32[1,512]{1,0:T(1,128)}) custom-call(bf16[384,512]{1,0:T(8,128)(2,1)} %get-tuple-element.12.refs_0_, bf16[384,512]{1,0:T(8,128)(2,1)} %get-tuple-element.13.refs_1_, bf16[384,512]{1,0:T(8,128)(2,1)} %get-tuple-element.14.refs_2_, ...), custom_call_target="tpu_custom_call" | custom-call | tf_op jit(solution)/shard_map/store_results/pallas_call | solution.py:539

commit v5 on v4

--- a/solution.py
+++ b/solution.py
@@ -95,7 +95,7 @@
     qg_ref, kg_ref, vg_ref, gain_out,
     q, k, v, g, w, a_hi, a_lo, p_hi, p_lo, out, grad, cols, q_t,
     loc, inbox, gsend, ginbox, csend, carry,
-    hsend, hinbox, nsend, ninbox, tsend, tinbox,
+    hsend, hinbox, ninbox, tsend, tinbox,
     in_sem, st_s, st_r, gr_s, gr_r, ca_s, ca_r, hd_s, hd_r, ng_s, ng_r, nt_s, nt_r,
 ):
     heads, length, n_seq, n_head, groups, reach = shape
@@ -146,8 +146,15 @@
 
     for o in range(1, heads):
         greet(seq=base + lax.rem(pos + o, heads))
-    for o in range(1, groups):
-        greet(seq=lax.rem(z + o, groups) * heads + pos)
+    for d in range(1, reach + 1):
+        @pl.when(z >= d)
+        def _(d=d):
+            greet(seq=me - d * heads)
+
+        @pl.when(z + d < groups)
+        def _(d=d):
+            greet(seq=me + d * heads)
+
     for o in range(1, n_head):
         greet(head=lax.rem(hx + o, n_head))
 
@@ -188,7 +195,10 @@
         for m in members:
             local_state(m)
         if i == 0:
-            pl.semaphore_wait(barrier, (heads - 1) + (groups - 1) + (n_head - 1))
+            near_groups = 0
+            for d in range(1, reach + 1):
+                near_groups += lax.div(z + groups - d, groups) + lax.div(2 * groups - 1 - z - d, groups)
+            pl.semaphore_wait(barrier, near_groups + (heads - 1) + (n_head - 1))
         post(0, members)
     local_state(pos)
 
@@ -400,25 +410,40 @@
         part = inbox[1, 0, 0, ROWS:]
         for p in range(1, heads):
             part = part + inbox[1, p, 0, ROWS:]
-        nsend[...] = part
-        ninbox[z] = part
-        for o in range(1, groups):
-            other = lax.rem(z + o, groups)
-            remote(nsend, ninbox.at[z], ng_s.at[o], ng_r.at[z], seq=other * heads + pos).start()
-
-    def whole_gain():
-        for o in range(1, groups):
-            other = lax.rem(z + o, groups)
-            remote(nsend, ninbox.at[other], ng_s.at[o], ng_r.at[other], seq=other * heads + pos).wait_recv()
-        part = ninbox[0]
-        for i in range(1, groups):
-            part = part + ninbox[i]
         tsend[...] = part
         tinbox[pos] = part
-        for p in range(heads):
-            @pl.when(p != pos)
-            def _(p=p):
-                remote(tsend, tinbox.at[pos], nt_s.at[p], nt_r.at[pos], seq=base + p).start()
+        for m in peers:
+            remote(tsend, tinbox.at[pos], nt_s.at[m], nt_r.at[pos], seq=base + m).start()
+
+    def pass_gain(far, action):
+        for t, source, there in ((0, z - far, z + 1), (1, z + far, z - 1)):
+            ok = (source >= 0) & (there < groups) if t == 0 else (source < groups) & (there >= 0)
+
+            @pl.when(ok)
+            def _(t=t, source=source, there=there):
+                action(remote(
+                    ninbox.at[source], ninbox.at[source], ng_s.at[t, far], ng_r.at[source], seq=there * heads + pos
+                ))
+
+    def take_gain(far):
+        for ok, source, there in ((z >= far, z - far, z - 1), (z + far < groups, z + far, z + 1)):
+            @pl.when(ok)
+            def _(source=source, there=there):
+                remote(
+                    ninbox.at[source], ninbox.at[source], ng_s.at[0, far], ng_r.at[source], seq=there * heads + pos
+                ).wait_recv()
+
+    def own_gain():
+        for m in peers:
+            remote(tsend, tinbox.at[m], nt_s.at[m], nt_r.at[m], seq=base + m).wait_recv()
+        rows = [tinbox[h, 2:3] for h in range(heads)]
+        rows += [jnp.zeros((1, HEAD_DIM), F32)] * (8 - heads)
+        ninbox[z] = cat(rows, 0)
+        pass_gain(0, lambda copy: copy.start())
+
+    def move_gain(far):
+        take_gain(far)
+        pass_gain(far, lambda copy: copy.start())
 
     def for_queries(h):
         lanes = pl.ds(h * HEAD_DIM, HEAD_DIM)
@@ -432,7 +457,8 @@
     def for_values(h):
         g[h] = under(turned(grad[h]), a_hi, a_lo, h)
 
-    steps = chunks(gather_group, 1) + [group_gain] + chunks(carry_out, 1) + [whole_gain]
+    steps = chunks(gather_group, 1) + [group_gain] + chunks(carry_out, 1)
+    steps += [own_gain] + [functools.partial(move_gain, far) for far in range(1, reach + 1)]
     weave(each(mix) + each(for_queries) + each(for_keys) + each(for_values), steps, heads)
     for m in [pos] + peers[::-1]:
         if m is not pos:
@@ -440,12 +466,13 @@
         state = carried(1, m)
         kg_ref[:, lanes_of(m)] = (out[m] + cols[1, m] * square_by_cols(split(v[m]), state)).astype(BF16)
         vg_ref[:, lanes_of(m)] = (g[m] + cols[1, m] * square_by_rows(split(k[m]), state)).astype(BF16)
-    for p in range(heads):
-        @pl.when(p != pos)
-        def _(p=p):
-            remote(tsend, tinbox.at[p], nt_s.at[p], nt_r.at[p], seq=base + p).wait_recv()
+    for far in range(reach + 1, groups):
+        move_gain(far)
+    part = ninbox[0]
+    for i in range(1, groups):
+        part = part + ninbox[i]
     for h in range(heads):
-        gain_out[:, h * HEAD_DIM : (h + 1) * HEAD_DIM] = tinbox[h, 2:3]
+        gain_out[:, h * HEAD_DIM : (h + 1) * HEAD_DIM] = part[h : h + 1]
 
     for t in range(2):
         for c in range(CHUNKS):
@@ -460,13 +487,10 @@
                 on_group(t, d, c, lambda copy: copy.wait_send())
     for o in range(1, n_head):
         remote(hsend, hinbox.at[hx], hd_s.at[o], hd_r.at[hx], head=lax.rem(hx + o, n_head)).wait_send()
-    for o in range(1, groups):
-        other = lax.rem(z + o, groups)
-        remote(nsend, ninbox.at[z], ng_s.at[o], ng_r.at[z], seq=other * heads + pos).wait_send()
-    for p in range(heads):
-        @pl.when(p != pos)
-        def _(p=p):
-            remote(tsend, tinbox.at[pos], nt_s.at[p], nt_r.at[pos], seq=base + p).wait_send()
+    for far in range(groups):
+        pass_gain(far, lambda copy: copy.wait_send())
+    for m in peers:
+        remote(tsend, tinbox.at[pos], nt_s.at[m], nt_r.at[pos], seq=base + m).wait_send()
 
 
 def store(*refs):
@@ -516,7 +540,6 @@
             pltpu.VMEM((2, heads, CHUNKS, ROWS, HEAD_DIM), F32),
             pltpu.VMEM((8, length), F32),
             pltpu.VMEM((n_head, 8, length), F32),
-            pltpu.VMEM((8, HEAD_DIM), F32),
             pltpu.VMEM((groups, 8, HEAD_DIM), F32),
             pltpu.VMEM((8, HEAD_DIM), F32),
             pltpu.VMEM((heads, 8, HEAD_DIM), F32),
@@ -525,7 +548,7 @@
             dma((2, reach, CHUNKS)), dma((2, reach, CHUNKS)),
             dma((2, heads, CHUNKS)), dma((2, heads, CHUNKS)),
             dma((n_head,)), dma((n_head,)),
-            dma((groups,)), dma((groups,)),
+            dma((2, groups)), dma((groups,)),
             dma((heads,)), dma((heads,)),
         ],
         compiler_params=pltpu.CompilerParams(

time: 41.3 us -> 46.1 us (1.12)
  Pallas kernels: 40.5 us -> 45.3 us
    pallas_call x1, Pallas kernels: 38.2 us -> 43.1 us  [body(): pl.pallas_call(functools.partial(kernel, shape), out_shape=(jax.ShapeDtyp...]
where the time goes in v5:
time: 46.1 us; the launch traced here: 46 us
  Pallas kernels  45.3 us (98%)
  between operations  0.64 us (1%)
    pallas_call x1, Pallas kernels, body(): pl.pallas_call(functools.partial(kernel, shape), out_shape=(jax.ShapeDtyp...  43.1 us
    pallas_call x1, Pallas kernels, body(): pl.pallas_call(store, out_shape=tuple((jax.ShapeDtypeStruct(x.shape, x.dt...  2.28 us

profile of v5, /device:TPU:0, one launch (start us, length us, event | category | flops | bytes accessed | tf_op | source)
XLA Modules:
  0.0 46.0 jit_solution(2508094749681076068)
XLA Ops:
  0.6 43.1 %decayed_attention_grad.1 = (bf16[384,512]{1,0:T(8,128)(2,1)}, bf16[384,512]{1,0:T(8,128)(2,1)}, bf16[384,512]{1,0:T(8,128)(2,1)}, f32[1,512]{1,0:T(1,128)}) custom-call(f32[384,512]{1,0:T(8,128)} %q_hbm.1, f32[384,512]{1,0:T(8,128)} %k_hbm.1, f32[384,512]{1,0:T(8,128)} %v_hbm.1, f32[384,512]{1,0:T(8,128)} %g_hbm.1, f32[1,512]{1,0:T(1,128)} %bitcast.2, ...), custom_call_target="tpu_custom_call" | custom-call | tf_op jit(solution)/shard_map/decayed_attention_grad/pallas_call | solution.py:518
  43.7 2.3 %store_results.1 = (bf16[384,512]{1,0:T(8,128)(2,1)}, bf16[384,512]{1,0:T(8,128)(2,1)}, bf16[384,512]{1,0:T(8,128)(2,1)}, f32[1,512]{1,0:T(1,128)}) custom-call(bf16[384,512]{1,0:T(8,128)(2,1)} %get-tuple-element.12.refs_0_, bf16[384,512]{1,0:T(8,128)(2,1)} %get-tuple-element.13.refs_1_, bf16[384,512]{1,0:T(8,128)(2,1)} %get-tuple-element.14.refs_2_, ...), custom_call_target="tpu_custom_call" | custom-call | tf_op jit(solution)/shard_map/store_results/pallas_call | solution.py:562

commit v6 on v4

--- a/solution.py
+++ b/solution.py
@@ -92,11 +92,11 @@
 
 def kernel(
     shape, q_hbm, k_hbm, v_hbm, g_hbm, gain_ref, rates, seg_ref,
-    qg_ref, kg_ref, vg_ref, gain_out,
+    qg_hbm, kg_hbm, vg_hbm, gain_out, qg_ref, kg_ref, vg_ref,
     q, k, v, g, w, a_hi, a_lo, p_hi, p_lo, out, grad, cols, q_t,
     loc, inbox, gsend, ginbox, csend, carry,
     hsend, hinbox, nsend, ninbox, tsend, tinbox,
-    in_sem, st_s, st_r, gr_s, gr_r, ca_s, ca_r, hd_s, hd_r, ng_s, ng_r, nt_s, nt_r,
+    in_sem, out_sem, st_s, st_r, gr_s, gr_r, ca_s, ca_r, hd_s, hd_r, ng_s, ng_r, nt_s, nt_r,
 ):
     heads, length, n_seq, n_head, groups, reach = shape
     me = lax.axis_index("seq")
@@ -132,6 +132,10 @@
     for i in (2, 3):
         for m in range(heads):
             load(i, m).start()
+
+    def keep(i, h):
+        src, dst = ((qg_ref, qg_hbm), (kg_ref, kg_hbm), (vg_ref, vg_hbm))[i]
+        return pltpu.make_async_copy(src.at[:, lanes_of(h)], dst.at[:, lanes_of(h)], out_sem.at[i, h])
 
     def remote(src, dst, ss, rs, **where):
         return pltpu.make_async_remote_copy(
@@ -425,6 +429,7 @@
         part = by_rows(p_hi, p_lo, h, split(k[h]))
         part = part + cols[0, h] * square_by_cols(split(grad[h]), carried(0, h))
         qg_ref[:, lanes] = part.astype(BF16)
+        keep(0, h).start()
 
     def for_keys(h):
         out[h] = under(q_t[h], p_hi, p_lo, h)
@@ -439,7 +444,9 @@
             wait_carry(1, m)
         state = carried(1, m)
         kg_ref[:, lanes_of(m)] = (out[m] + cols[1, m] * square_by_cols(split(v[m]), state)).astype(BF16)
+        keep(1, m).start()
         vg_ref[:, lanes_of(m)] = (g[m] + cols[1, m] * square_by_rows(split(k[m]), state)).astype(BF16)
+        keep(2, m).start()
     for p in range(heads):
         @pl.when(p != pos)
         def _(p=p):
@@ -447,6 +454,9 @@
     for h in range(heads):
         gain_out[:, h * HEAD_DIM : (h + 1) * HEAD_DIM] = tinbox[h, 2:3]
 
+    for i in range(3):
+        for h in range(heads):
+            keep(i, h).wait()
     for t in range(2):
         for c in range(CHUNKS):
             for m in peers:
@@ -470,11 +480,15 @@
 
 
 def store(*refs):
-    sem = refs[-1]
-    copies = [pltpu.make_async_copy(refs[i], refs[4 + i], sem.at[i]) for i in range(4)]
-    for copy in copies:
+    ins, outs, held, sem = refs[:4], refs[4:8], refs[8:12], refs[12]
+    here = [pltpu.make_async_copy(ins[i], held[i], sem.at[0, i]) for i in range(4)]
+    away = [pltpu.make_async_copy(held[i], outs[i], sem.at[1, i]) for i in range(4)]
+    for copy in here:
         copy.start()
-    for copy in copies:
+    for first, second in zip(here, away):
+        first.wait()
+        second.start()
+    for copy in away:
         copy.wait()
 
 
@@ -500,8 +514,9 @@
             jax.ShapeDtypeStruct((1, width), F32),
         ),
         in_specs=[any_spec] * 4 + [vmem, pl.BlockSpec(memory_space=pltpu.SMEM), vmem],
-        out_specs=(vmem,) * 4,
+        out_specs=(any_spec,) * 3 + (vmem,),
         scratch_shapes=[
+            pltpu.VMEM((length, width), BF16), pltpu.VMEM((length, width), BF16), pltpu.VMEM((length, width), BF16),
             pltpu.VMEM(tok, F32), pltpu.VMEM(tok, F32), pltpu.VMEM(tok, F32), pltpu.VMEM(tok, F32),
             pltpu.VMEM(sq, F32),
             pltpu.VMEM(sq, BF16), pltpu.VMEM(sq, BF16), pltpu.VMEM(sq, BF16), pltpu.VMEM(sq, BF16),
@@ -520,7 +535,7 @@
             pltpu.VMEM((groups, 8, HEAD_DIM), F32),
             pltpu.VMEM((8, HEAD_DIM), F32),
             pltpu.VMEM((heads, 8, HEAD_DIM), F32),
-            dma((4, heads)),
+            dma((4, heads)), dma((3, heads)),
             dma((2, heads, CHUNKS)), dma((2, heads, CHUNKS)),
             dma((2, reach, CHUNKS)), dma((2, reach, CHUNKS)),
             dma((2, heads, CHUNKS)), dma((2, heads, CHUNKS)),
@@ -539,9 +554,9 @@
     outs = pl.pallas_call(
         store,
         out_shape=tuple(jax.ShapeDtypeStruct(x.shape, x.dtype) for x in outs),
-        in_specs=[vmem] * 4,
+        in_specs=[any_spec] * 4,
         out_specs=(any_spec,) * 4,
-        scratch_shapes=[dma((4,))],
+        scratch_shapes=[pltpu.VMEM(x.shape, x.dtype) for x in outs] + [dma((2, 4))],
         compiler_params=pltpu.CompilerParams(vmem_limit_bytes=VMEM_BYTES),
         name="store_results",
     )(*outs)

time: 41.3 us -> 41.4 us (level)
  no operation moved by 1% of the time
where the time goes in v6:
time: 41.4 us; the launch traced here: 41.2 us
  Pallas kernels  40.5 us (98%)
  between operations  0.64 us (2%)
    pallas_call x1, Pallas kernels, body(): pl.pallas_call(functools.partial(kernel, shape), out_shape=(jax.ShapeDtyp...  38.5 us
    pallas_call x1, Pallas kernels, body(): pl.pallas_call(store, out_shape=tuple((jax.ShapeDtypeStruct(x.shape, x.dt...  2.07 us

profile of v6, /device:TPU:0, one launch (start us, length us, event | category | flops | bytes accessed | tf_op | source)
XLA Modules:
  0.0 41.2 jit_solution(8489089015064095318)
XLA Ops:
  0.6 38.5 %decayed_attention_grad.1 = (bf16[384,512]{1,0:T(8,128)(2,1)}, bf16[384,512]{1,0:T(8,128)(2,1)}, bf16[384,512]{1,0:T(8,128)(2,1)}, f32[1,512]{1,0:T(1,128)}) custom-call(f32[384,512]{1,0:T(8,128)} %q_hbm.1, f32[384,512]{1,0:T(8,128)} %k_hbm.1, f32[384,512]{1,0:T(8,128)} %v_hbm.1, f32[384,512]{1,0:T(8,128)} %g_hbm.1, f32[1,512]{1,0:T(1,128)} %bitcast.2, ...), custom_call_target="tpu_custom_call" | custom-call | tf_op jit(solution)/shard_map/decayed_attention_grad/pallas_call | solution.py:508
  39.1 2.1 %store_results.1 = (bf16[384,512]{1,0:T(8,128)(2,1)}, bf16[384,512]{1,0:T(8,128)(2,1)}, bf16[384,512]{1,0:T(8,128)(2,1)}, f32[1,512]{1,0:T(1,128)}) custom-call(bf16[384,512]{1,0:T(8,128)(2,1)} %get-tuple-element.12.refs_0_, bf16[384,512]{1,0:T(8,128)(2,1)} %get-tuple-element.13.refs_1_, bf16[384,512]{1,0:T(8,128)(2,1)} %get-tuple-element.14.refs_2_, ...), custom_call_target="tpu_custom_call" | custom-call | tf_op jit(solution)/shard_map/store_results/pallas_call | solution.py:554
